TPU v7x, 256 devices: a whole 4x4x8 slice. The times are simulated.
256 devices in a mesh: dp: 2 (over x_hi), ctx: 16 (over z, core), tp: 8 (over x_lo, y).
Axes of the slice: x: 4 (x_hi: 2, x_lo: 2; x = x_hi * 2 + x_lo), y: 4, z: 8, core: 2. Of those that a mesh axis runs over, the one named last changes fastest.
Arguments:
- tokens: bfloat16 [8192, 3072], P(('dp', 'ctx'), 'tp'), parts along dimension 0, may hold values from -20 to 20
- tangent: bfloat16 [8192, 3072], P(('dp', 'ctx'), 'tp'), parts along dimension 0, may hold values from -6 to 6
- w_query: bfloat16 [3072, 3072], P(None, 'tp'), may hold values from -0.109375 to 0.109375
- w_key: bfloat16 [3072, 3072], P(None, 'tp'), may hold values from -0.109375 to 0.109375
- w_value: bfloat16 [3072, 3072], P(None, 'tp'), may hold values from -0.109375 to 0.109375
- w_output: bfloat16 [3072, 3072], P('tp'), may hold values from -0.4375 to 0.4375
Outputs:
- layer_out: bfloat16 [8192, 3072], P(('dp', 'ctx'), 'tp'), parts along dimension 0
- layer_tangent: bfloat16 [8192, 3072], P(('dp', 'ctx'), 'tp'), parts along dimension 0
There are 2 independent parts, one for each index of `dp`. A program takes and returns all parts, laid end to end along the dimension named above; an argument that names none is the same for every part. Nothing has to cross between parts.
All inputs are finite; a program needn't handle non-finite values.
Results may differ from a plain program's by a relative error of at most 0.02.
The roundings to bfloat16 on the way count: a program that leaves them out, or rounds other values in their place, can miss the bound.
Values may be sent and summed in bfloat16 or wider, within the bound.
A program may use at most 128 MiB of HBM per device.

v0:
```python
import jax
import jax.numpy as jnp
from jax import lax
from jax.sharding import PartitionSpec as P

HEAD_DIM = 128


def split_heads(block_rows):
    count = block_rows.shape[0]
    return block_rows.reshape(count, block_rows.shape[1] // HEAD_DIM, HEAD_DIM)


def score_pair(query, q_dot, key_piece, kdot_piece):
    factor = HEAD_DIM ** (-0.5)
    scores = (
        jnp.einsum("qhd,khd->hqk", query, key_piece, preferred_element_type=jnp.float32) * factor
    )
    s_dot = (
        jnp.einsum("qhd,khd->hqk", q_dot, key_piece, preferred_element_type=jnp.float32)
        + jnp.einsum("qhd,khd->hqk", query, kdot_piece, preferred_element_type=jnp.float32)
    ) * factor
    return (scores, s_dot)


def body(tokens, tangent, w_query, w_key, w_value, w_output):
    rows = tokens.shape[0]
    local = w_query.shape[1]
    heads_here = local // HEAD_DIM
    empty = jnp.zeros((rows, local), jnp.float32)
    totals = (empty,) * 6
    pieces = (
        lax.all_gather(tokens, "tp", axis=1, tiled=True),
        lax.all_gather(tangent, "tp", axis=1, tiled=True),
    )
    outputs = []
    for source_index in range(2):
        for weight_index, weight_rows in enumerate((w_query, w_key, w_value)):
            total = totals[3 * source_index + weight_index]
            outputs.append(
                jnp.dot(pieces[source_index], weight_rows, preferred_element_type=jnp.float32)
            )
    projected = tuple(outputs)
    query, key, value, q_dot, k_dot, v_dot = [p.astype(jnp.bfloat16) for p in projected]
    query_h = split_heads(query)
    qdot_h = split_heads(q_dot)
    low = jnp.full((heads_here, rows), -1e30, jnp.float32)
    pieces = (
        lax.all_gather(key, "ctx", axis=0, tiled=True),
        lax.all_gather(value, "ctx", axis=0, tiled=True),
    )
    key_piece = split_heads(pieces[0])
    value_piece = split_heads(pieces[1])
    factor = HEAD_DIM ** (-0.5)
    scores = (
        jnp.einsum("qhd,khd->hqk", query_h, key_piece, preferred_element_type=jnp.float32) * factor
    )
    new_top = jnp.maximum(low, jnp.max(scores, axis=-1))
    expo = jnp.exp(scores - new_top[:, :, None])
    total = jnp.sum(expo, axis=-1)
    acc_v = jnp.einsum(
        "hqk,khd->hqd", expo.astype(jnp.bfloat16), value_piece, preferred_element_type=jnp.float32
    )
    top, total, acc_v = (new_top, total, acc_v)
    pieces = (
        lax.all_gather(key, "ctx", axis=0, tiled=True),
        lax.all_gather(value, "ctx", axis=0, tiled=True),
        lax.all_gather(k_dot, "ctx", axis=0, tiled=True),
        lax.all_gather(v_dot, "ctx", axis=0, tiled=True),
    )
    key_piece = split_heads(pieces[0])
    value_piece = split_heads(pieces[1])
    kdot_piece = split_heads(pieces[2])
    vdot_piece = split_heads(pieces[3])
    scores, s_dot = score_pair(query_h, qdot_h, key_piece, kdot_piece)
    expo = jnp.exp(scores - top[:, :, None])
    product = expo * s_dot
    tilt = jnp.sum(product, axis=-1)
    acc_t = jnp.einsum(
        "hqk,khd->hqd",
        product.astype(jnp.bfloat16),
        value_piece,
        preferred_element_type=jnp.float32,
    ) + jnp.einsum(
        "hqk,khd->hqd", expo.astype(jnp.bfloat16), vdot_piece, preferred_element_type=jnp.float32
    )
    tilt, acc_t = (tilt, acc_t)
    total_e = total[:, :, None]
    attended = acc_v / total_e
    att_dot = (acc_t - tilt[:, :, None] / total_e * acc_v) / total_e
    attended = attended.transpose(1, 0, 2).reshape(rows, local).astype(jnp.bfloat16)
    att_dot = att_dot.transpose(1, 0, 2).reshape(rows, local).astype(jnp.bfloat16)
    out_term = jnp.dot(attended, w_output, preferred_element_type=jnp.float32)
    tangent_term = jnp.dot(att_dot, w_output, preferred_element_type=jnp.float32)
    layer_out, layer_tangent = (
        lax.psum_scatter(
            out_term.astype(jnp.bfloat16), "tp", scatter_dimension=1, tiled=True
        ).astype(jnp.float32),
        lax.psum_scatter(
            tangent_term.astype(jnp.bfloat16), "tp", scatter_dimension=1, tiled=True
        ).astype(jnp.float32),
    )
    return (layer_out.astype(jnp.bfloat16), layer_tangent.astype(jnp.bfloat16))


def solution(mesh):
    placed = (
        P(("dp", "ctx"), "tp"),
        P(("dp", "ctx"), "tp"),
        P(None, "tp"),
        P(None, "tp"),
        P(None, "tp"),
        P("tp", None),
    )
    return jax.shard_map(
        body,
        mesh=mesh,
        in_specs=placed,
        out_specs=(P(("dp", "ctx"), "tp"), P(("dp", "ctx"), "tp")),
        check_vma=False,
    )
```

profile of v0, /device:TPU:4, one launch (start us, length us, event | category | flops | bytes accessed | tf_op | source)
XLA Modules:
  0.0 379.8 jit_solution(13743628954953732858)
XLA Ops:
  7.2 0.0 copy-start
  7.2 0.0 all-gather.7.cloned.1.call-start
  7.2 0.7 all-gather.7.cloned.1.call-update
  7.9 0.0 all-gather.13.cloned.1.call-start
  8.0 0.7 all-gather.13.cloned.1.call-update
  8.7 0.0 all-gather.9.cloned.1.call-start
  8.7 46.8 %all-gather.7.cloned.1.call-done = bf16[256,3072]{1,0:T(8,128)(2,1)} async-done(((bf16[256,384]{1,0:T(8,128)(2,1)}), bf16[256,3072]{1,0:T(8,128)(2,1)}) %all-gather.7.cloned.1.call-update) | async-done | bytes 1572880 | tf_op jit(solution)/shard_map/all_gather | solution.py:33
  55.5 3.8 %convolution_convert_fusion.6 = bf16[256,384]{1,0:T(8,128)(2,1)} fusion(bf16[256,3072]{1,0:T(8,128)(2,1)} %all-gather.7.cloned.1.call-done, bf16[3072,384]{1,0:T(8,128)(2,1)} %param.9), kind=kOutput, calls=%fused_computation.17 | convolution fusion | flops 604078080 | bytes 4128768 | tf_op jit(solution)/shard_map/dot_general | solution.py:41
  59.3 0.0 all-gather.9.cloned.1.call-update
  59.3 0.0 all-gather.15.cloned.1.call-start
  59.4 40.1 %all-gather.13.cloned.1.call-done = bf16[256,3072]{1,0:T(8,128)(2,1)} async-done(((bf16[256,384]{1,0:T(8,128)(2,1)}), bf16[256,3072]{1,0:T(8,128)(2,1)}) %all-gather.13.cloned.1.call-update) | async-done | bytes 1572880 | tf_op jit(solution)/shard_map/all_gather | solution.py:34
  99.4 3.8 %convolution_convert_fusion.3 = bf16[256,384]{1,0:T(8,128)(2,1)} fusion(bf16[256,3072]{1,0:T(8,128)(2,1)} %all-gather.13.cloned.1.call-done, bf16[3072,384]{1,0:T(8,128)(2,1)} %param.9), kind=kOutput, calls=%fused_computation.14 | convolution fusion | flops 604078080 | bytes 4128768 | tf_op jit(solution)/shard_map/dot_general | solution.py:41
  103.2 0.0 all-gather.15.cloned.1.call-update
  103.2 0.0 all-gather.11.cloned.1.call-start
  103.3 3.8 %convolution_convert_fusion.5 = bf16[256,384]{1,0:T(8,128)(2,1)} fusion(bf16[256,3072]{1,0:T(8,128)(2,1)} %all-gather.7.cloned.1.call-done, bf16[3072,384]{1,0:T(8,128)(2,1)} %param.10), kind=kOutput, calls=%fused_computation.16 | convolution fusion | flops 604078080 | bytes 4128768 | tf_op jit(solution)/shard_map/dot_general | solution.py:41
  107.1 0.0 all-gather.11.cloned.1.call-update
  107.1 0.0 all-gather.17.cloned.1.call-start
  107.2 3.8 %convolution_convert_fusion.2 = bf16[256,384]{1,0:T(8,128)(2,1)} fusion(bf16[256,3072]{1,0:T(8,128)(2,1)} %all-gather.13.cloned.1.call-done, bf16[3072,384]{1,0:T(8,128)(2,1)} %param.10), kind=kOutput, calls=%fused_computation.13 | convolution fusion | flops 604078080 | bytes 4128768 | tf_op jit(solution)/shard_map/dot_general | solution.py:41
  111.0 0.0 all-gather.17.cloned.1.call-update
  111.0 0.0 reduce-scatter.9.cloned.1.call-start
  111.1 3.3 convolution_convert_fusion.7
  114.3 0.1 copy.29
  114.5 3.1 convolution_convert_fusion.4
  117.6 0.1 copy.34
  117.7 24.5 %all-gather.9.cloned.1.call-done = bf16[4096,384]{1,0:T(8,128)(2,1)} async-done(((bf16[256,384]{1,0:T(8,128)(2,1)}), bf16[4096,384]{1,0:T(8,128)(2,1)}) %all-gather.9.cloned.1.call-update) | async-done | bytes 3145744 | tf_op jit(solution)/shard_map/all_gather | solution.py:49
  142.2 4.8 %copy.30 = bf16[4096,384]{0,1:T(8,128)(2,1)} copy(bf16[4096,384]{1,0:T(8,128)(2,1)} %all-gather.9.cloned.1.call-done) | data formatting | bytes 6291456 | tf_op jit(solution)/shard_map/all_gather | solution.py:49
  147.0 36.5 %all-gather.15.cloned.1.call-done = bf16[4096,384]{1,0:T(8,128)(2,1)} async-done(((bf16[256,384]{1,0:T(8,128)(2,1)}), bf16[4096,384]{1,0:T(8,128)(2,1)}) %all-gather.15.cloned.1.call-update) | async-done | bytes 3145744 | tf_op jit(solution)/shard_map/all_gather | solution.py:68
  183.6 4.7 %copy.37 = bf16[4096,384]{0,1:T(8,128)(2,1)} copy(bf16[4096,384]{1,0:T(8,128)(2,1)} %all-gather.15.cloned.1.call-done) | data formatting | bytes 6291456 | tf_op jit(solution)/shard_map/all_gather | solution.py:68
  188.3 37.1 %all-gather.11.cloned.1.call-done = bf16[4096,384]{1,0:T(8,128)(2,1)} async-done(((bf16[256,384]{1,0:T(8,128)(2,1)}), bf16[4096,384]{1,0:T(8,128)(2,1)}) %all-gather.11.cloned.1.call-update) | async-done | bytes 3145744 | tf_op jit(solution)/shard_map/all_gather | solution.py:50
  225.5 4.7 %copy.33 = bf16[4096,384]{0,1:T(8,128)(2,1)} copy(bf16[4096,384]{1,0:T(8,128)(2,1)} %all-gather.11.cloned.1.call-done) | data formatting | bytes 6291456 | tf_op jit(solution)/shard_map/all_gather | solution.py:50
  230.2 0.0 copy-start.2
  230.2 4.0 %multiply_reduce_fusion = (f32[3,256]{1,0:T(4,128)S(1)}, f32[3,256,4096]{2,1,0:T(8,128)S(1)}) fusion(bf16[256,3,128]{0,2,1:T(8,128)(2,1)S(1)} %bitcast.60, bf16[4096,3,128]{0,2,1:T(8,128)(2,1)} %bitcast.52), kind=kOutput, calls=%fused_computation.2 | convolution fusion | flops 811597056 | bytes 15928320 | tf_op jit(solution)/shard_map/qhd,khd->hqk/dot_general | solution.py:56
  234.2 0.0 copy-start.1
  234.2 0.0 copy-done.2
  234.2 6.8 %fusion.13 = f32[3,256,4096]{2,1,0:T(8,128)} fusion(bf16[256,3,128]{0,2,1:T(8,128)(2,1)S(1)} %bitcast.62, bf16[4096,3,128]{0,2,1:T(8,128)(2,1)S(1)} %bitcast.53), kind=kOutput, calls=%fused_computation.27 | convolution fusion | flops 805306368 | bytes 15925248 | tf_op jit(solution)/shard_map/qhd,khd->hqk/dot_general | solution.py:20
  241.0 1.5 copy-done.1
  242.5 2.2 fusion
  244.7 0.0 copy-start.3
  244.7 12.1 %fusion.12 = (f32[3,256]{1,0:T(4,128)S(1)}, bf16[3,256,4096]{2,1,0:T(8,128)(2,1)S(1)}) fusion(f32[3,256,4096]{2,1,0:T(8,128)} %fusion.13, bf16[256,3,128]{0,2,1:T(8,128)(2,1)S(1)} %bitcast.61, bf16[4096,3,128]{0,2,1:T(8,128)(2,1)} %bitcast.54, f32[3,256]{1,0:T(4,128)S(1)} %broadcast_maximum_fusion, f32[3,256,4096]{2,1,0:T(8,128)} %copy-done.1), kind=kOutput, calls=%fused_computation.26 | convolution fusion | flops 827325696 | bytes 34805760 | tf_op jit(solution)/shard_map/qhd,khd->hqk/dot_general | solution.py:21
  256.8 0.0 copy-done.3
  256.8 2.2 fusion.2
  259.0 6.2 %divide_convert_fusion = (bf16[256,3,128]{0,2,1:T(8,128)(2,1)S(1)}, f32[256,3,128]{0,2,1:T(8,128)S(1)}) fusion(f32[256,3]{0,1:T(4,128)S(1)} %bitcast.67, bf16[4096,3,128]{0,2,1:T(8,128)(2,1)S(1)} %bitcast.58, f32[3,256,4096]{2,1,0:T(8,128)} %copy-done.1, f32[3,256]{1,0:T(4,128)S(1)} %broadcast_maximum_fusion), kind=kOutput, calls=%fused_computation.21 | convolution fusion | flops 814940160 | bytes 16324608 | tf_op jit(solution)/shard_map/hqk,khd->hqd/dot_general | solution.py:61
  265.3 1.5 all-gather.17.cloned.1.call-done
  266.8 4.8 %copy.40 = bf16[4096,384]{0,1:T(8,128)(2,1)} copy(bf16[4096,384]{1,0:T(8,128)(2,1)} %all-gather.17.cloned.1.call-done) | data formatting | bytes 6291456 | tf_op jit(solution)/shard_map/all_gather | solution.py:69
  271.6 8.1 %fusion.7 = bf16[256,3,128]{0,2,1:T(8,128)(2,1)S(1)} fusion(f32[3,256,128]{1,2,0:T(8,128)S(1)} %fusion.2, bf16[4096,3,128]{0,2,1:T(8,128)(2,1)} %bitcast.59, f32[3,256,4096]{2,1,0:T(8,128)} %copy-done.1, f32[3,256]{1,0:T(4,128)S(1)} %broadcast_maximum_fusion, f32[256,3,128]{0,2,1:T(8,128)S(1)} %get-tuple-element.5, f32[256,3]{0,1:T(4,128)S(1)} %bitcast_divide_fusion, ...), kind=kOutput, calls=%fused_computation.20 | convolution fusion | flops 815235072 | bytes 16720896 | tf_op jit(solution)/shard_map/hqk,khd->hqd/dot_general | solution.py:84
  279.7 0.0 copy-done
  279.7 2.2 convolution_convert_fusion
  281.8 2.6 copy.49
  284.4 0.0 reduce-scatter.9.cloned.1.call-update
  284.5 0.0 reduce-scatter.7.cloned.1.call-start
  284.5 2.2 convolution_convert_fusion.1
  286.7 2.6 copy.47
  289.3 0.0 reduce-scatter.7.cloned.1.call-update
  289.3 37.1 %reduce-scatter.9.cloned.1.call-done = bf16[384,256]{1,0:T(8,128)(2,1)} async-done(((bf16[3072,256]{1,0:T(8,128)(2,1)}), bf16[384,256]{1,0:T(8,128)(2,1)}) %reduce-scatter.9.cloned.1.call-update) | async-done | bytes 196624
  326.4 1.7 copy.50
  328.1 43.1 %reduce-scatter.7.cloned.1.call-done = bf16[384,256]{1,0:T(8,128)(2,1)} async-done(((bf16[3072,256]{1,0:T(8,128)(2,1)}), bf16[384,256]{1,0:T(8,128)(2,1)}) %reduce-scatter.7.cloned.1.call-update) | async-done | bytes 196624
  371.3 1.7 copy.48
  (2 shorter events, 0.0 us)
Async XLA Ops:
  7.2 272.5 %copy-start = (bf16[384,3072]{1,0:T(8,128)(2,1)S(1)}, bf16[384,3072]{1,0:T(8,128)(2,1)}, u32[]{:S(2)}) copy-start(bf16[384,3072]{1,0:T(8,128)(2,1)} %param.11) | copy-start | bytes 7077892
  7.2 48.3 %all-gather.7.cloned.1.call-start = ((), (), s32[]{:S(2)}) async-start(), calls=%async_computation.2 | async-start | bytes 1769472 | tf_op jit(solution)/shard_map/all_gather | solution.py:33
  7.9 91.5 %all-gather.13.cloned.1.call-start = ((), (), s32[]{:S(2)}) async-start(), calls=%async_computation.5 | async-start | bytes 1769472 | tf_op jit(solution)/shard_map/all_gather | solution.py:34
  8.7 133.6 %all-gather.9.cloned.1.call-start = ((), (), s32[]{:S(2)}) async-start(), calls=%async_computation.3 | async-start | bytes 3342336 | tf_op jit(solution)/shard_map/all_gather | solution.py:49
  59.3 124.3 %all-gather.15.cloned.1.call-start = ((), (), s32[]{:S(2)}) async-start(), calls=%async_computation.6 | async-start | bytes 3342336 | tf_op jit(solution)/shard_map/all_gather | solution.py:68
  103.2 122.2 %all-gather.11.cloned.1.call-start = ((), (), s32[]{:S(2)}) async-start(), calls=%async_computation.4 | async-start | bytes 3342336 | tf_op jit(solution)/shard_map/all_gather | solution.py:50
  107.1 159.7 %all-gather.17.cloned.1.call-start = ((), (), s32[]{:S(2)}) async-start(), calls=%async_computation.7 | async-start | bytes 3342336 | tf_op jit(solution)/shard_map/all_gather | solution.py:69
  111.0 215.4 %reduce-scatter.9.cloned.1.call-start = ((), (), s32[]{:S(2)}) async-start(), calls=%async_computation.9 | async-start | bytes 1769472
  230.2 4.0 %copy-start.2 = (bf16[4096,384]{0,1:T(8,128)(2,1)S(1)}, bf16[4096,384]{0,1:T(8,128)(2,1)}, u32[]{:S(2)}) copy-start(bf16[4096,384]{0,1:T(8,128)(2,1)} %copy.30) | copy-start | bytes 9437188
  234.2 8.3 %copy-start.1 = (f32[3,256,4096]{2,1,0:T(8,128)}, f32[3,256,4096]{2,1,0:T(8,128)S(1)}, u32[]{:S(2)}) copy-start(f32[3,256,4096]{2,1,0:T(8,128)S(1)} %get-tuple-element.3) | copy-start | bytes 37748740
  244.7 12.1 %copy-start.3 = (bf16[4096,384]{0,1:T(8,128)(2,1)S(1)}, bf16[4096,384]{0,1:T(8,128)(2,1)}, u32[]{:S(2)}) copy-start(bf16[4096,384]{0,1:T(8,128)(2,1)} %copy.33) | copy-start | bytes 9437188
  284.5 86.8 %reduce-scatter.7.cloned.1.call-start = ((), (), s32[]{:S(2)}) async-start(), calls=%async_computation.8 | async-start | bytes 1769472
Sparse Core Ops, SparseCore 0:
  9.8 45.6 all-gather.6
  57.3 42.0 all-gather.12
  101.8 40.3 all-gather.8
  143.9 39.5 all-gather.14
  185.8 39.5 all-gather.10
  227.1 39.5 all-gather.16
  284.6 41.7 reduce-scatter.8
  328.9 42.2 reduce-scatter.6
where the time goes:
time: 380 us
  waiting for transfers between devices  268 us (71%)
  matrix products  65.3 us (17%)
  local copies, waits for them, and re-layouts  29.5 us (8%)
  between operations  14.3 us (4%)
    unnamed x10, waiting for transfers between devices  81.7 us
    all_gather x1, waiting for transfers between devices, body(): lax.all_gather(tokens, 'tp', axis=1, tiled=True)  46.8 us
    all_gather x1, waiting for transfers between devices, body(): lax.all_gather(tangent, 'tp', axis=1, tiled=True)  40.1 us
    all_gather x1, waiting for transfers between devices, body(): lax.all_gather(value, 'ctx', axis=0, tiled=True)  37.1 us
    all_gather x1, waiting for transfers between devices, body(): lax.all_gather(k_dot, 'ctx', axis=0, tiled=True)  36.5 us
    all_gather x1, waiting for transfers between devices, body(): lax.all_gather(key, 'ctx', axis=0, tiled=True)  24.5 us
    dot_general x6, matrix products, body(): jnp.dot(pieces[source_index], weight_rows, preferred_element_type=jnp.flo...  21.6 us
    dot_general x1, matrix products, score_pair(): jnp.einsum('qhd,khd->hqk', query, kdot_piece, preferred_element_type=jnp....  12.1 us
  transfers between devices with their start and end apart: 8, of which 8 were waited for; matrix products, arithmetic and copies ran while one was open for 20% of the time, Pallas kernels for 0%

commit v1 on v0

v1 whole, which is shorter than its diff:
```python
import jax
import jax.numpy as jnp
from jax import lax
from jax.experimental import pallas as pl
from jax.experimental.pallas import tpu as pltpu
from jax.sharding import PartitionSpec as P

MESH = pl.DeviceIdType.MESH
HD = 128
HEADS_HERE = 3
ROWS = 256
COLS = 384
D = 3072
CTX = 16
TP = 8
LANES_KV = 2 * HD
FACTOR = HD ** (-0.5)
LOG2E = 1.4426950408889634
BF16 = jnp.bfloat16
F32 = jnp.float32

GATHERS = ((0, 0, 64), (0, 64, 64), (0, 128, 64), (0, 192, 64), (1, 0, 128), (1, 128, 128))
N_T = 4
N_ITEMS = N_T + HEADS_HERE


def dot_nt(a, b):
    return lax.dot_general(a, b, (((1,), (1,)), ((), ())), preferred_element_type=F32)


def dot_nn(a, b):
    return jnp.dot(a, b, preferred_element_type=F32)


def kernel(
    tok, tan, wq, wk, wv, wo, out_ref, outd_ref,
    xg, wbuf, kvt, kvd, qcat, wt, at, acc_e, acc_w, stat, total,
    loc_sem, g_send, g_recv, z_send, z_recv, s_recv, a_send, a_recv, p_send, p_recv,
):
    dp, ctx, tp = lax.axis_index("dp"), lax.axis_index("ctx"), lax.axis_index("tp")
    core = lax.rem(ctx, 2)
    x, y = tp // 4, lax.rem(tp, 4)
    y_up, y_down, y_far = lax.rem(y + 1, 4), lax.rem(y + 3, 4), lax.rem(y + 2, 4)
    other = 1 - x
    zp = (dp, lax.rem(ctx + 2, CTX), tp)
    zm = (dp, lax.rem(ctx + 14, CTX), tp)
    sib = (dp, ctx + 1 - 2 * core, tp)

    def plane(xx, yy):
        return (dp, ctx, xx * 4 + yy)

    xn, yp, ym = plane(other, y), plane(x, y_up), plane(x, y_down)
    s_x, s_p, s_m = other * 4 + y, x * 4 + y_up, x * 4 + y_down
    s_xp, s_xm = other * 4 + y_up, other * 4 + y_down
    s_f, s_xf = x * 4 + y_far, other * 4 + y_far
    peers = (xn, yp, ym, plane(other, y_up), plane(other, y_down), plane(x, y_far), plane(other, y_far))

    def cols(slot, width):
        return pl.ds(pl.multiple_of(slot * width, 128), width)

    local = [
        pltpu.make_async_copy(tok, xg.at[0, :, cols(tp, COLS)], loc_sem.at[0]),
        pltpu.make_async_copy(tan, xg.at[1, :, cols(tp, COLS)], loc_sem.at[1]),
    ]
    for h in range(HEADS_HERE):
        for j, w in enumerate((wk, wv)):
            local.append(
                pltpu.make_async_copy(
                    w.at[:, pl.ds(h * HD, HD)],
                    wbuf.at[:, pl.ds(h * LANES_KV + j * HD, HD)],
                    loc_sem.at[2 + 2 * h + j],
                )
            )
    local.append(
        pltpu.make_async_copy(wq, wbuf.at[:, pl.ds(3 * LANES_KV, COLS)], loc_sem.at[8])
    )
    local.append(
        pltpu.make_async_copy(
            wo.at[:, pl.ds(core * 64, 64), cols(tp, COLS)], wt.at[:, tp, core], loc_sem.at[9]
        )
    )
    for c in local:
        c.start()

    barrier = pltpu.get_barrier_semaphore()
    greet = (zp, zm, sib) + peers
    for dev in greet:
        pl.semaphore_signal(barrier, inc=1, device_id=dev, device_id_type=MESH)
    pl.semaphore_wait(barrier, len(greet))

    sent = []

    def send(src, dst, ssem, rsem, dev):
        c = pltpu.make_async_remote_copy(
            src_ref=src, dst_ref=dst, send_sem=ssem, recv_sem=rsem, device_id=dev, device_id_type=MESH
        )
        c.start()
        sent.append(c)

    def arrived(ref, ssem, rsem, dev):
        pltpu.make_async_remote_copy(
            src_ref=ref, dst_ref=ref, send_sem=ssem, recv_sem=rsem, device_id=dev, device_id_type=MESH
        ).wait_recv()

    class Gather:
        def __init__(self, view, ssem, rsem, n):
            self.view, self.ssem, self.rsem, self.n = view, ssem, rsem, n

        def go(self, slot, part, j, dev):
            ref = self.part(slot, part)
            send(ref, ref, self.ssem(j), self.rsem(j), dev)

        def part(self, slot, part):
            half = self.n // 2
            lo, n = ((0, self.n), (0, half), (half, half))[part]
            return self.view(slot, lo, n)

        def got(self, slot, part, j):
            arrived(self.part(slot, part), self.ssem(j), self.rsem(j), xn)

        def start(self):
            self.go(tp, 0, 0, xn)
            self.go(tp, 0, 1, yp)
            self.go(tp, 0, 2, ym)

        def step1(self):
            self.got(s_x, 0, 0)
            self.go(s_x, 0, 3, yp)
            self.go(s_x, 0, 4, ym)
            self.got(s_m, 0, 1)
            self.go(s_m, 1, 5, yp)
            self.got(s_p, 0, 2)
            self.go(s_p, 2, 7, ym)

        def step2(self):
            self.got(s_xm, 0, 3)
            self.go(s_xm, 1, 6, yp)
            self.got(s_xp, 0, 4)
            self.go(s_xp, 2, 8, ym)

        def finish(self):
            self.got(s_f, 1, 5)
            self.got(s_xf, 1, 6)
            self.got(s_f, 2, 7)
            self.got(s_xf, 2, 8)

    def acts(g):
        a, r0, n = GATHERS[g]
        return Gather(
            lambda slot, lo, cnt: xg.at[a, pl.ds(r0 + lo, cnt), cols(slot, COLS)],
            lambda j: g_send.at[g, j], lambda j: g_recv.at[g, j], n,
        )

    def heads_out(h):
        return Gather(
            lambda slot, lo, cnt: at.at[h, pl.ds(lo, cnt), cols(slot, HD)],
            lambda j: a_send.at[h, j], lambda j: a_recv.at[h, j], 2 * ROWS,
        )

    def piece(i, c, part):
        if i < N_T:
            _, r0, n = GATHERS[i]
            if part == 0:
                return kvt.at[c, :, :, pl.ds(r0, n)]
            return kvt.at[c, :, part - 1, pl.ds(r0, n)]
        if part == 0:
            return kvd.at[i - N_T, c]
        return kvd.at[i - N_T, c, part - 1]

    def minus(d):
        return lax.rem(ctx + CTX - 2 * d, CTX)

    def plus(d):
        return lax.rem(ctx + 2 * d, CTX)

    def ring_send(i, c, part, j, dev):
        ref = piece(i, c, part)
        send(ref, ref, z_send.at[i, j], z_recv.at[i, j], dev)

    def sib_send(i, c, j):
        ref = piece(i, c, 0)
        send(ref, ref, z_send.at[i, 8 + j], s_recv.at[i, j], sib)

    def ring_got(i, c, part, j):
        arrived(piece(i, c, part), z_send.at[i, j], z_recv.at[i, j], zp)

    def own(i):
        ring_send(i, ctx, 0, 0, zp)
        ring_send(i, ctx, 0, 4, zm)
        sib_send(i, ctx, 0)

    def hop(i, d):
        if d < 4:
            ring_got(i, minus(d), 0, d - 1)
            ring_send(i, minus(d), 0 if d < 3 else 1, d, zp)
            ring_got(i, plus(d), 0, 4 + d - 1)
            ring_send(i, plus(d), 0 if d < 3 else 2, 4 + d, zm)
            sib_send(i, minus(d), 2 * d - 1)
            sib_send(i, plus(d), 2 * d)
        else:
            ring_got(i, minus(4), 1, 3)
            ring_got(i, plus(4), 2, 7)
            sib_send(i, plus(4), 7)

    def sib_got(i, j):
        d = (j + 1) // 2
        pair = ctx + 1 - 2 * core
        c = lax.rem(pair + CTX - 2 * d, CTX) if j % 2 else lax.rem(pair + 2 * d, CTX)
        arrived(piece(i, c, 0), z_send.at[i, 8 + j], s_recv.at[i, j], sib)

    def keys_values_t(g):
        _, r0, n = GATHERS[g]
        for h in range(HEADS_HERE):
            res = dot_nn(xg[0, pl.ds(r0, n), :], wbuf[:, pl.ds(h * LANES_KV, LANES_KV)]).astype(BF16)
            kvt[ctx, h, 0, pl.ds(r0, n), :] = res[:, :HD]
            kvt[ctx, h, 1, pl.ds(r0, n), :] = res[:, HD:]

    def keys_values_d(h):
        res = dot_nn(xg[1], wbuf[:, pl.ds(h * LANES_KV, LANES_KV)]).astype(BF16)
        kvd[h, ctx, 0] = res[:, :HD]
        kvd[h, ctx, 1] = res[:, HD:]

    def queries(a):
        res = dot_nn(xg[a], wbuf[:, pl.ds(3 * LANES_KV, COLS)]).astype(BF16)
        for h in range(HEADS_HERE):
            qcat[h, :, pl.ds((1 - a) * HD, HD)] = res[:, h * HD : (h + 1) * HD]

    def attend(h, chip, first):
        c0 = chip * 2
        kk = kvt[pl.ds(c0, 2), h, 0].reshape(2 * ROWS, HD)
        vv = kvt[pl.ds(c0, 2), h, 1].reshape(2 * ROWS, HD)
        kd = kvd[h, pl.ds(c0, 2), 0].reshape(2 * ROWS, HD)
        vd = kvd[h, pl.ds(c0, 2), 1].reshape(2 * ROWS, HD)
        kcat = jnp.concatenate([kk, kd], axis=1)
        vcat = jnp.concatenate([vv, vd], axis=1)
        for blk in range(2):
            rows = pl.ds(blk * 128, 128)
            qq = qcat[h, rows, :]
            s = dot_nt(qq[:, HD:], kk)
            sd = dot_nt(qq, kcat)
            top = jnp.max(s, axis=1, keepdims=True)
            if not first:
                old = stat[h, 0, rows, :][:, :1]
                top = jnp.maximum(old, top)
            p = jnp.exp2((s - top) * (FACTOR * LOG2E))
            w = p * sd
            l_new = jnp.sum(p, axis=1, keepdims=True)
            t_new = jnp.sum(w, axis=1, keepdims=True)
            e_new = dot_nn(p.astype(BF16), vcat)
            w_new = dot_nn(w.astype(BF16), vv)
            if not first:
                keep = jnp.exp2((old - top) * (FACTOR * LOG2E))
                l_new += stat[h, 1, rows, :][:, :1] * keep
                t_new += stat[h, 2, rows, :][:, :1] * keep
                e_new += acc_e[h, rows, :] * keep
                w_new += acc_w[h, rows, :] * keep
            stat[h, 0, rows, :] = jnp.broadcast_to(top, (128, HD))
            stat[h, 1, rows, :] = jnp.broadcast_to(l_new, (128, HD))
            stat[h, 2, rows, :] = jnp.broadcast_to(t_new, (128, HD))
            acc_e[h, rows, :] = e_new
            acc_w[h, rows, :] = w_new

    me_chip = ctx // 2

    def stage(h, d):
        i = N_T + h
        if h == 0:
            for t in range(N_T):
                for j in ((0,) if d == 0 else ((2 * d - 1, 2 * d) if d < 4 else (7,))):
                    sib_got(t, j)
        for j in ((0,) if d == 0 else ((2 * d - 1, 2 * d) if d < 4 else (7,))):
            sib_got(i, j)
        if d == 0:
            attend(h, me_chip, True)
        elif d == 4:
            attend(h, lax.rem(me_chip + 4, 8), False)
        else:
            def both(k, carry):
                attend(h, lax.rem(me_chip + 8 - d + 2 * d * k, 8), False)
                return carry
            lax.fori_loop(0, 2, both, 0)

    def close(h):
        l = stat[h, 1]
        num_v = acc_e[h, :, pl.ds(0, HD)]
        att = num_v / l
        num_t = acc_w[h] * FACTOR + acc_e[h, :, pl.ds(HD, HD)]
        dot_part = (num_t - (stat[h, 2] * FACTOR / l) * num_v) / l
        at[h, pl.ds(0, ROWS), cols(tp, HD)] = att.astype(BF16)
        at[h, pl.ds(ROWS, ROWS), cols(tp, HD)] = dot_part.astype(BF16)

    def project(h):
        res = dot_nn(at[h], wt[h].reshape(TP * HD, COLS))
        if h == 0:
            total[...] = res
        elif h == 1:
            total[...] += res
        else:
            res = (total[...] + res).astype(BF16)
            out_ref[...] = res[:ROWS]
            outd_ref[...] = res[ROWS:]

    G = [acts(g) for g in range(len(GATHERS))]
    A = [heads_out(h) for h in range(HEADS_HERE)]

    def make_t(g):
        G[g].finish()
        keys_values_t(g)
        own(g)

    local[0].wait()
    G[0].start()
    G[1].start()
    G[0].step1()
    G[1].step1()
    G[0].step2()
    G[2].start()
    G[1].step2()
    for c in local[2:8]:
        c.wait()
    make_t(0)
    G[2].step1()
    G[3].start()
    make_t(1)
    G[2].step2()
    G[3].step1()
    hop(0, 1)
    make_t(2)
    G[3].step2()
    hop(1, 1)
    local[1].wait()
    G[4].start()
    hop(0, 2)
    make_t(3)
    G[5].start()
    hop(2, 1)
    hop(1, 2)
    hop(0, 3)
    local[8].wait()
    queries(0)
    G[4].step1()
    hop(3, 1)
    hop(2, 2)
    hop(1, 3)
    G[5].step1()
    hop(0, 4)
    hop(3, 2)
    hop(2, 3)
    G[4].step2()
    hop(1, 4)
    G[5].step2()
    G[4].finish()
    G[5].finish()
    keys_values_d(0)
    own(4)
    hop(3, 3)
    local[9].wait()
    slots = (s_x, s_p, s_m, s_xp, s_xm, s_f, s_xf)
    for j, dev in enumerate(peers):
        send(
            wo.at[:, pl.ds(core * 64, 64), cols(slots[j], COLS)], wt.at[:, tp, core],
            p_send.at[j], p_recv.at[j], dev,
        )
    keys_values_d(1)
    own(5)
    hop(2, 4)
    hop(4, 1)
    hop(3, 4)
    queries(1)
    stage(0, 0)
    keys_values_d(2)
    hop(5, 1)
    hop(4, 2)
    own(6)
    stage(0, 1)
    stage(1, 0)
    hop(4, 3)
    hop(5, 2)
    stage(0, 2)
    hop(6, 1)
    hop(4, 4)
    stage(1, 1)
    hop(5, 3)
    stage(0, 3)
    stage(0, 4)
    close(0)
    A[0].start()
    stage(2, 0)
    hop(6, 2)
    back = (s_x, s_m, s_p, s_xm, s_xp, s_f, s_xf)
    for j in range(len(peers)):
        arrived(wt.at[:, back[j], core], p_send.at[j], p_recv.at[j], peers[j])
    send(wt.at[:, :, core], wt.at[:, :, core], p_send.at[7], p_recv.at[7], sib)
    hop(5, 4)
    stage(1, 2)
    stage(2, 1)
    A[0].step1()
    stage(1, 3)
    hop(6, 3)
    stage(1, 4)
    close(1)
    A[1].start()
    A[0].step2()
    stage(2, 2)
    A[1].step1()
    hop(6, 4)
    stage(2, 3)
    A[1].step2()
    stage(2, 4)
    close(2)
    A[2].start()
    arrived(wt.at[:, :, 1 - core], p_send.at[7], p_recv.at[7], sib)
    A[0].finish()
    project(0)
    A[2].step1()
    A[1].finish()
    project(1)
    A[2].step2()
    A[2].finish()
    project(2)
    for c in sent:
        c.wait_send()


def body(tokens, tangent, w_query, w_key, w_value, w_output):
    wo = w_output.reshape(HEADS_HERE, HD, D)
    hbm = pl.BlockSpec(memory_space=pl.ANY)
    vmem = pl.BlockSpec(memory_space=pltpu.VMEM)
    dma = pltpu.SemaphoreType.DMA
    n_g = len(GATHERS)
    layer_out, layer_tangent = pl.pallas_call(
        kernel,
        out_shape=[jax.ShapeDtypeStruct((ROWS, COLS), BF16)] * 2,
        in_specs=[hbm] * 6,
        out_specs=[vmem] * 2,
        scratch_shapes=[
            pltpu.VMEM((2, ROWS, D), BF16),
            pltpu.VMEM((D, 3 * COLS), BF16),
            pltpu.VMEM((CTX, HEADS_HERE, 2, ROWS, HD), BF16),
            pltpu.VMEM((HEADS_HERE, CTX, 2, ROWS, HD), BF16),
            pltpu.VMEM((HEADS_HERE, ROWS, 2 * HD), BF16),
            pltpu.VMEM((HEADS_HERE, TP, 2, 64, COLS), BF16),
            pltpu.VMEM((HEADS_HERE, 2 * ROWS, TP * HD), BF16),
            pltpu.VMEM((HEADS_HERE, ROWS, 2 * HD), F32),
            pltpu.VMEM((HEADS_HERE, ROWS, HD), F32),
            pltpu.VMEM((HEADS_HERE, 3, ROWS, HD), F32),
            pltpu.VMEM((2 * ROWS, COLS), F32),
            dma((10,)),
            dma((n_g, 9)),
            dma((n_g, 9)),
            dma((N_ITEMS, 16)),
            dma((N_ITEMS, 8)),
            dma((N_ITEMS, 8)),
            dma((HEADS_HERE, 9)),
            dma((HEADS_HERE, 9)),
            dma((8,)),
            dma((8,)),
        ],
        compiler_params=pltpu.CompilerParams(
            collective_id=0, has_side_effects=True, vmem_limit_bytes=56 << 20
        ),
        cost_estimate=pl.CostEstimate(flops=12_000_000_000, bytes_accessed=40_000_000, transcendentals=3_200_000),
    )(tokens, tangent, w_query, w_key, w_value, wo)
    return layer_out, layer_tangent


def solution(mesh):
    placed = (
        P(("dp", "ctx"), "tp"),
        P(("dp", "ctx"), "tp"),
        P(None, "tp"),
        P(None, "tp"),
        P(None, "tp"),
        P("tp", None),
    )
    return jax.shard_map(
        body,
        mesh=mesh,
        in_specs=placed,
        out_specs=(P(("dp", "ctx"), "tp"), P(("dp", "ctx"), "tp")),
        check_vma=False,
    )
```

time: 380 us -> 124 us (0.33)
  waiting for transfers between devices: 268 us -> 0 us
  Pallas kernels: 0 us -> 120 us
  matrix products: 65.3 us -> 0 us
  local copies, waits for them, and re-layouts: 29.5 us -> 3.25 us
  between operations: 14.3 us -> 0.64 us
    all_gather x6 -> x0, waiting for transfers between devices: 186 us -> none  [the longest x1 46.8 us: body(): lax.all_gather(tokens, 'tp', axis=1, tiled=True)]
    pallas_call x0 -> x1, Pallas kernels: none -> 120 us  [body(): pl.pallas_call(kernel, out_shape=[jax.ShapeDtypeStruct((ROWS, COLS), BF16...]
    unnamed x10 -> x0, waiting for transfers between devices: 81.7 us -> none
    dot_general x14 -> x0, matrix products: 65.3 us -> none  [the longest x6 21.6 us: body(): jnp.dot(pieces[source_index], weight_rows, preferred_element_type=jnp.flo...]
    all_gather x4 -> x0, local copies, waits for them, and re-layouts: 19 us -> none  [the longest x1 4.78 us: body(): lax.all_gather(key, 'ctx', axis=0, tiled=True)]
    unnamed x12 -> x2, local copies, waits for them, and re-layouts: 10.2 us -> 3.25 us
  transfers between devices with their start and end apart: 8 -> 0, of which waited for: 8 -> 0; matrix products, arithmetic and copies ran while one was open for 20% -> 0% of each run, Pallas kernels for 0% -> 0%
where the time goes in v1:
time: 124 us
  Pallas kernels  120 us (97%)
  local copies, waits for them, and re-layouts  3.25 us (3%)
    pallas_call x1, Pallas kernels, body(): pl.pallas_call(kernel, out_shape=[jax.ShapeDtypeStruct((ROWS, COLS), BF16...  120 us
    unnamed x2, local copies, waits for them, and re-layouts  3.25 us

profile of v1, /device:TPU:4, one launch (start us, length us, event | category | flops | bytes accessed | tf_op | source)
XLA Modules:
  0.0 124.1 jit_solution(9583042661302234290)
XLA Ops:
  0.6 120.2 %shard_map.77 = (bf16[256,384]{1,0:T(8,128)(2,1)}, bf16[256,384]{1,0:T(8,128)(2,1)}) custom-call(bf16[256,384]{1,0:T(8,128)(2,1)} %tok.1, bf16[256,384]{1,0:T(8,128)(2,1)} %tan.1, bf16[3072,384]{1,0:T(8,128)(2,1)} %wq.1, bf16[3072,384]{1,0:T(8,128)(2,1)} %wk.1, bf16[3072,384]{1,0:T(8,128)(2,1)} %wv.1, bf16[3,128,3072]{2,1,0:T(8,128)(2,1)} %bitcast.1), custom_call_target="tpu_custom_call" | custom-call | flops 12000000000 | bytes 40000000 | tf_op jit(solution)/shard_map/pallas_call | solution.py:431
  120.9 1.6 %copy.10 = bf16[256,384]{1,0:T(8,128)(2,1)} copy(bf16[256,384]{1,0:T(8,128)(2,1)} %get-tuple-element.4) | data formatting | bytes 393216
  122.5 1.6 %copy.11 = bf16[256,384]{1,0:T(8,128)(2,1)} copy(bf16[256,384]{1,0:T(8,128)(2,1)} %get-tuple-element.5) | data formatting | bytes 393216

commit v2 on v1

v2 whole, which is shorter than its diff:
```python
import jax
import jax.numpy as jnp
from jax import lax
from jax.experimental import pallas as pl
from jax.experimental.pallas import tpu as pltpu
from jax.sharding import PartitionSpec as P

MESH = pl.DeviceIdType.MESH
HD = 128
HEADS_HERE = 3
ROWS = 256
COLS = 384
D = 3072
CTX = 16
TP = 8
LANES_KV = 2 * HD
FACTOR = HD ** (-0.5)
LOG2E = 1.4426950408889634
BF16 = jnp.bfloat16
F32 = jnp.float32

GATHERS = ((0, 0, 32), (0, 32, 32), (0, 64, 64), (0, 128, 64), (0, 192, 64), (1, 0, 128), (1, 128, 128))
DIRECT = (False, False, False, False, False, False, False)
DIRECT_OUT = (True, True, True, False)
N_T = 5
N_ITEMS = N_T + HEADS_HERE


def dot_nt(a, b):
    return lax.dot_general(a, b, (((1,), (1,)), ((), ())), preferred_element_type=F32)


def dot_nn(a, b):
    return jnp.dot(a, b, preferred_element_type=F32)


def kernel(
    tok, tan, wq, wk, wv, wo, out_ref, outd_ref,
    xg, wbuf, kvt, kvd, qcat, wt, at, acc_v, acc_w, stat, total,
    loc_sem, g_send, g_recv, z_send, z_recv, s_recv, a_send, a_recv, p_send, p_recv,
):
    dp, ctx, tp = lax.axis_index("dp"), lax.axis_index("ctx"), lax.axis_index("tp")
    core = lax.rem(ctx, 2)
    x, y = tp // 4, lax.rem(tp, 4)
    y_up, y_down, y_far = lax.rem(y + 1, 4), lax.rem(y + 3, 4), lax.rem(y + 2, 4)
    other = 1 - x
    zp = (dp, lax.rem(ctx + 2, CTX), tp)
    zm = (dp, lax.rem(ctx + 14, CTX), tp)
    sib = (dp, ctx + 1 - 2 * core, tp)

    def plane(xx, yy):
        return (dp, ctx, xx * 4 + yy)

    xn, yp, ym = plane(other, y), plane(x, y_up), plane(x, y_down)
    xyp, xym = plane(other, y_up), plane(other, y_down)
    s_x, s_p, s_m = other * 4 + y, x * 4 + y_up, x * 4 + y_down
    s_xp, s_xm = other * 4 + y_up, other * 4 + y_down
    s_f, s_xf = x * 4 + y_far, other * 4 + y_far
    peers = (xn, yp, ym, xyp, xym, plane(x, y_far), plane(other, y_far))

    slots = (s_x, s_p, s_m, s_xp, s_xm, s_f, s_xf)
    back = (s_x, s_m, s_p, s_xm, s_xp, s_f, s_xf)

    def cols(slot, width):
        return pl.ds(pl.multiple_of(slot * width, 128), width)

    local = [
        pltpu.make_async_copy(tok, xg.at[0, :, cols(tp, COLS)], loc_sem.at[0]),
        pltpu.make_async_copy(tan, xg.at[1, :, cols(tp, COLS)], loc_sem.at[1]),
    ]
    for h in range(HEADS_HERE):
        for j, w in enumerate((wk, wv)):
            local.append(
                pltpu.make_async_copy(
                    w.at[:, pl.ds(h * HD, HD)],
                    wbuf.at[:, pl.ds(h * LANES_KV + j * HD, HD)],
                    loc_sem.at[2 + 2 * h + j],
                )
            )
    local.append(
        pltpu.make_async_copy(wq, wbuf.at[:, pl.ds(3 * LANES_KV, COLS)], loc_sem.at[8])
    )
    local.append(
        pltpu.make_async_copy(
            wo.at[:, pl.ds(core * 64, 64), cols(tp, COLS)], wt.at[:, tp, core], loc_sem.at[9]
        )
    )
    for c in local:
        c.start()

    barrier = pltpu.get_barrier_semaphore()
    greet = (zp, zm, sib) + peers
    for dev in greet:
        pl.semaphore_signal(barrier, inc=1, device_id=dev, device_id_type=MESH)
    pl.semaphore_wait(barrier, len(greet))

    sent = []

    def send(src, dst, ssem, rsem, dev):
        c = pltpu.make_async_remote_copy(
            src_ref=src, dst_ref=dst, send_sem=ssem, recv_sem=rsem, device_id=dev, device_id_type=MESH
        )
        c.start()
        sent.append(c)

    def arrived(ref, ssem, rsem, dev):
        pltpu.make_async_remote_copy(
            src_ref=ref, dst_ref=ref, send_sem=ssem, recv_sem=rsem, device_id=dev, device_id_type=MESH
        ).wait_recv()

    class Gather:
        def __init__(self, view, ssem, rsem, n, direct):
            self.view, self.ssem, self.rsem, self.n, self.direct = view, ssem, rsem, n, direct

        def part(self, slot, part):
            half = self.n // 2
            lo, n = ((0, self.n), (0, half), (half, half))[part]
            return self.view(slot, lo, n)

        def go(self, slot, part, j, dev):
            ref = self.part(slot, part)
            send(ref, ref, self.ssem(j), self.rsem(j), dev)

        def got(self, slot, part, j):
            arrived(self.part(slot, part), self.ssem(j), self.rsem(j), xn)

        def start(self):
            for j, dev in enumerate(peers if self.direct else peers[:5]):
                self.go(tp, 0, j, dev)

        def fwd(self, k):
            self.got(back[1 + k], 0, 1 + k)
            self.go(back[1 + k], 1 + k % 2, 5 + k, (yp, ym)[k % 2])

        def finish(self):
            if self.direct:
                for j in range(len(peers)):
                    self.got(back[j], 0, j)
            else:
                self.got(s_x, 0, 0)
                for k, slot in enumerate((s_f, s_f, s_xf, s_xf)):
                    self.got(slot, 1 + k % 2, 5 + k)

    def acts(g):
        a, r0, n = GATHERS[g]
        return Gather(
            lambda slot, lo, cnt: xg.at[a, pl.ds(r0 + lo, cnt), cols(slot, COLS)],
            lambda j: g_send.at[g, j], lambda j: g_recv.at[g, j], n, DIRECT[g],
        )

    def heads_out(h):
        if h < HEADS_HERE:
            view = lambda slot, lo, cnt: at.at[h, pl.ds(ROWS + lo, cnt), cols(slot, HD)]
        else:
            view = lambda slot, lo, cnt: at.at[:, pl.ds(lo, cnt), cols(slot, HD)]
        return Gather(view, lambda j: a_send.at[h, j], lambda j: a_recv.at[h, j], ROWS, DIRECT_OUT[h])

    def piece(i, c, part):
        if i < N_T:
            _, r0, n = GATHERS[i]
            if part == 0:
                return kvt.at[c, :, :, pl.ds(r0, n)]
            return kvt.at[c, :, part - 1, pl.ds(r0, n)]
        if part == 0:
            return kvd.at[i - N_T, c]
        return kvd.at[i - N_T, c, part - 1]

    def minus(d):
        return lax.rem(ctx + CTX - 2 * d, CTX)

    def plus(d):
        return lax.rem(ctx + 2 * d, CTX)

    def ring_send(i, c, part, j, dev):
        ref = piece(i, c, part)
        send(ref, ref, z_send.at[i, j], z_recv.at[i, j], dev)

    def sib_send(i, c, j):
        ref = piece(i, c, 0)
        send(ref, ref, z_send.at[i, 8 + j], s_recv.at[i, j], sib)

    def ring_got(i, c, part, j):
        arrived(piece(i, c, part), z_send.at[i, j], z_recv.at[i, j], zp)

    def own(i):
        ring_send(i, ctx, 0, 0, zp)
        ring_send(i, ctx, 0, 4, zm)
        sib_send(i, ctx, 0)

    def hop(i, d):
        if d < 4:
            ring_got(i, minus(d), 0, d - 1)
            ring_send(i, minus(d), 0 if d < 3 else 1, d, zp)
            ring_got(i, plus(d), 0, 4 + d - 1)
            ring_send(i, plus(d), 0 if d < 3 else 2, 4 + d, zm)
            sib_send(i, minus(d), 2 * d - 1)
            sib_send(i, plus(d), 2 * d)
        else:
            ring_got(i, minus(4), 1, 3)
            ring_got(i, plus(4), 2, 7)
            sib_send(i, plus(4), 7)

    def sib_got(i, j):
        d = (j + 1) // 2
        pair = ctx + 1 - 2 * core
        c = lax.rem(pair + CTX - 2 * d, CTX) if j % 2 else lax.rem(pair + 2 * d, CTX)
        arrived(piece(i, c, 0), z_send.at[i, 8 + j], s_recv.at[i, j], sib)

    def keys_values_t(g):
        _, r0, n = GATHERS[g]
        for h in range(HEADS_HERE):
            res = dot_nn(xg[0, pl.ds(r0, n), :], wbuf[:, pl.ds(h * LANES_KV, LANES_KV)]).astype(BF16)
            kvt[ctx, h, 0, pl.ds(r0, n), :] = res[:, :HD]
            kvt[ctx, h, 1, pl.ds(r0, n), :] = res[:, HD:]

    def keys_values_d(h):
        res = dot_nn(xg[1], wbuf[:, pl.ds(h * LANES_KV, LANES_KV)]).astype(BF16)
        kvd[h, ctx, 0] = res[:, :HD]
        kvd[h, ctx, 1] = res[:, HD:]

    def queries(a):
        res = dot_nn(xg[a], wbuf[:, pl.ds(3 * LANES_KV, COLS)]).astype(BF16)
        for h in range(HEADS_HERE):
            qcat[h, :, pl.ds((1 - a) * HD, HD)] = res[:, h * HD : (h + 1) * HD]

    def attend(h, chip, first):
        c0 = chip * 2
        kk = kvt[pl.ds(c0, 2), h, 0].reshape(2 * ROWS, HD)
        vv = kvt[pl.ds(c0, 2), h, 1].reshape(2 * ROWS, HD)
        for blk in range(2):
            rows = pl.ds(blk * 128, 128)
            s = dot_nt(qcat[h, rows, pl.ds(HD, HD)], kk)
            top = jnp.max(s, axis=1, keepdims=True)
            if not first:
                old = stat[h, 0, rows, :][:, :1]
                top = jnp.maximum(old, top)
            p = jnp.exp2((s - top) * (FACTOR * LOG2E))
            l_new = jnp.sum(p, axis=1, keepdims=True)
            v_new = dot_nn(p.astype(BF16), vv)
            if not first:
                keep = jnp.exp2((old - top) * (FACTOR * LOG2E))
                l_new += stat[h, 1, rows, :][:, :1] * keep
                v_new += acc_v[h, rows, :] * keep
            stat[h, 0, rows, :] = jnp.broadcast_to(top, (128, HD))
            stat[h, 1, rows, :] = jnp.broadcast_to(l_new, (128, HD))
            acc_v[h, rows, :] = v_new

    def attend_dot(h, chip, first):
        c0 = chip * 2
        kk = kvt[pl.ds(c0, 2), h, 0].reshape(2 * ROWS, HD)
        vv = kvt[pl.ds(c0, 2), h, 1].reshape(2 * ROWS, HD)
        kd = kvd[h, pl.ds(c0, 2), 0].reshape(2 * ROWS, HD)
        vd = kvd[h, pl.ds(c0, 2), 1].reshape(2 * ROWS, HD)
        kcat = jnp.concatenate([kk, kd], axis=1)
        for blk in range(2):
            rows = pl.ds(blk * 128, 128)
            qq = qcat[h, rows, :]
            s = dot_nt(qq[:, HD:], kk)
            sd = dot_nt(qq, kcat)
            p = jnp.exp2((s - stat[h, 0, rows, :][:, :1]) * (FACTOR * LOG2E))
            w = p * sd
            t_new = jnp.sum(w, axis=1, keepdims=True)
            w_new = dot_nn(w.astype(BF16), vv) * FACTOR + dot_nn(p.astype(BF16), vd)
            if not first:
                t_new += stat[h, 2, rows, :][:, :1]
                w_new += acc_w[h, rows, :]
            stat[h, 2, rows, :] = jnp.broadcast_to(t_new, (128, HD))
            acc_w[h, rows, :] = w_new

    me_chip = ctx // 2

    def arrivals(d):
        return (0,) if d == 0 else ((2 * d - 1, 2 * d) if d < 4 else (7,))

    def over(attending, h, d):
        if d == 0:
            attending(h, me_chip, True)
        elif d == 4:
            attending(h, lax.rem(me_chip + 4, 8), False)
        else:
            def both(k, carry):
                attending(h, lax.rem(me_chip + 8 - d + 2 * d * k, 8), False)
                return carry
            lax.fori_loop(0, 2, both, 0)

    def t_got(d):
        for j in arrivals(d):
            for t in range(N_T):
                sib_got(t, j)

    def d_got(h, d):
        for j in arrivals(d):
            sib_got(N_T + h, j)

    def stage(h, d):
        over(attend, h, d)

    def stage_dot(h, d):
        over(attend_dot, h, d)

    def close():
        for h in range(HEADS_HERE):
            at[h, pl.ds(0, ROWS), cols(tp, HD)] = (acc_v[h] / stat[h, 1]).astype(BF16)

    def close_dot(h):
        l = stat[h, 1]
        res = (acc_w[h] - (stat[h, 2] * FACTOR / l) * acc_v[h]) / l
        at[h, pl.ds(ROWS, ROWS), cols(tp, HD)] = res.astype(BF16)

    def project():
        res = jnp.zeros((ROWS, COLS), F32)
        for h in range(HEADS_HERE):
            res += dot_nn(at[h, pl.ds(0, ROWS), :], wt[h].reshape(TP * HD, COLS))
        out_ref[...] = res.astype(BF16)

    def project_dot(h):
        res = dot_nn(at[h, pl.ds(ROWS, ROWS), :], wt[h].reshape(TP * HD, COLS))
        if h > 0:
            res += total[...]
        if h < HEADS_HERE - 1:
            total[...] = res
        else:
            outd_ref[...] = res.astype(BF16)

    def weights_send(j):
        send(
            wo.at[:, pl.ds(core * 64, 64), cols(slots[j], COLS)], wt.at[:, tp, core],
            p_send.at[j], p_recv.at[j], peers[j],
        )

    def weights_share():
        for j in range(len(peers)):
            arrived(wt.at[:, back[j], core], p_send.at[j], p_recv.at[j], peers[j])
        local[9].wait()
        send(wt.at[:, :, core], wt.at[:, :, core], p_send.at[7], p_recv.at[7], sib)

    def weights_got():
        arrived(wt.at[:, :, 1 - core], p_send.at[7], p_recv.at[7], sib)

    G = [acts(g) for g in range(len(GATHERS))]
    A = [heads_out(h) for h in range(HEADS_HERE + 1)]

    def make_t(g):
        G[g].finish()
        keys_values_t(g)

    def kvw_wait():
        for c in local[2:8]:
            c.wait()

    def d_gathered():
        for g in range(N_T, len(GATHERS)):
            G[g].finish()

    local[0].wait()
    G[0].start()
    G[1].start()
    G[2].start()
    G[0].fwd(0)
    G[0].fwd(1)
    kvw_wait()
    G[1].fwd(0)
    G[1].fwd(1)
    G[0].fwd(2)
    G[3].start()
    G[0].fwd(3)
    G[2].fwd(0)
    G[2].fwd(1)
    G[1].fwd(2)
    G[1].fwd(3)
    G[4].start()
    G[3].fwd(1)
    G[2].fwd(2)
    G[3].fwd(0)
    G[2].fwd(3)
    make_t(0)
    own(0)
    make_t(1)
    G[4].fwd(0)
    G[3].fwd(2)
    G[4].fwd(1)
    own(1)
    local[1].wait()
    G[5].start()
    G[3].fwd(3)
    hop(0, 1)
    make_t(2)
    own(2)
    G[4].fwd(2)
    hop(1, 1)
    G[4].fwd(3)
    hop(0, 2)
    G[5].fwd(1)
    G[5].fwd(0)
    hop(2, 1)
    G[6].start()
    make_t(3)
    hop(1, 2)
    G[5].fwd(2)
    own(3)
    make_t(4)
    hop(0, 3)
    local[8].wait()
    queries(0)
    G[5].fwd(3)
    own(4)
    hop(2, 2)
    G[6].fwd(0)
    G[6].fwd(1)
    hop(1, 3)
    t_got(0)
    stage(0, 0)
    stage(1, 0)
    weights_send(0)
    stage(2, 0)
    hop(3, 1)
    G[6].fwd(2)
    hop(0, 4)
    weights_send(1)
    G[6].fwd(3)
    hop(4, 1)
    t_got(1)
    stage(0, 1)
    hop(1, 4)
    hop(2, 3)
    d_gathered()
    keys_values_d(0)
    keys_values_d(1)
    hop(3, 2)
    keys_values_d(2)
    queries(1)
    weights_send(2)
    stage(1, 1)
    hop(4, 2)
    hop(2, 4)
    stage(2, 1)
    weights_send(3)
    own(5)
    t_got(2)
    stage(0, 2)
    hop(3, 3)
    stage(1, 2)
    hop(4, 3)
    d_got(0, 0)
    weights_send(4)
    stage(2, 2)
    t_got(3)
    stage(0, 3)
    hop(5, 1)
    weights_send(5)
    stage(1, 3)
    hop(3, 4)
    stage(2, 3)
    hop(4, 4)
    own(6)
    d_got(0, 1)
    weights_send(6)
    t_got(4)
    stage(0, 4)
    hop(5, 2)
    d_got(1, 0)
    stage(1, 4)
    stage(2, 4)
    close()
    A[3].start()
    d_got(0, 2)
    stage_dot(0, 0)
    hop(6, 1)
    stage_dot(0, 1)
    stage_dot(0, 2)
    hop(5, 3)
    d_got(1, 1)
    stage_dot(1, 0)
    own(7)
    stage_dot(1, 1)
    A[3].fwd(0)
    A[3].fwd(1)
    hop(6, 2)
    d_got(2, 0)
    d_got(0, 3)
    stage_dot(0, 3)
    hop(5, 4)
    stage_dot(2, 0)
    d_got(1, 2)
    stage_dot(1, 2)
    A[3].fwd(2)
    hop(7, 1)
    d_got(0, 4)
    stage_dot(0, 4)
    close_dot(0)
    A[0].start()
    weights_share()
    hop(6, 3)
    d_got(2, 1)
    stage_dot(2, 1)
    A[3].fwd(3)
    hop(7, 2)
    weights_got()
    d_got(1, 3)
    stage_dot(1, 3)
    hop(6, 4)
    d_got(2, 2)
    stage_dot(2, 2)
    d_got(1, 4)
    stage_dot(1, 4)
    hop(7, 3)
    close_dot(1)
    A[1].start()
    A[0].finish()
    project_dot(0)
    A[3].finish()
    project()
    d_got(2, 3)
    stage_dot(2, 3)
    hop(7, 4)
    d_got(2, 4)
    stage_dot(2, 4)
    close_dot(2)
    A[2].start()
    A[1].finish()
    project_dot(1)
    A[2].finish()
    project_dot(2)
    for c in sent:
        c.wait_send()


def hand_on(a_ref, b_ref, c_ref, d_ref):
    c_ref[...] = a_ref[...]
    d_ref[...] = b_ref[...]


def body(tokens, tangent, w_query, w_key, w_value, w_output):
    wo = w_output.reshape(HEADS_HERE, HD, D)
    hbm = pl.BlockSpec(memory_space=pl.ANY)
    vmem = pl.BlockSpec(memory_space=pltpu.VMEM)
    dma = pltpu.SemaphoreType.DMA
    n_g = len(GATHERS)
    layer_out, layer_tangent = pl.pallas_call(
        kernel,
        out_shape=[jax.ShapeDtypeStruct((ROWS, COLS), BF16)] * 2,
        in_specs=[hbm] * 6,
        out_specs=[vmem] * 2,
        scratch_shapes=[
            pltpu.VMEM((2, ROWS, D), BF16),
            pltpu.VMEM((D, 3 * COLS), BF16),
            pltpu.VMEM((CTX, HEADS_HERE, 2, ROWS, HD), BF16),
            pltpu.VMEM((HEADS_HERE, CTX, 2, ROWS, HD), BF16),
            pltpu.VMEM((HEADS_HERE, ROWS, 2 * HD), BF16),
            pltpu.VMEM((HEADS_HERE, TP, 2, 64, COLS), BF16),
            pltpu.VMEM((HEADS_HERE, 2 * ROWS, TP * HD), BF16),
            pltpu.VMEM((HEADS_HERE, ROWS, HD), F32),
            pltpu.VMEM((HEADS_HERE, ROWS, HD), F32),
            pltpu.VMEM((HEADS_HERE, 3, ROWS, HD), F32),
            pltpu.VMEM((ROWS, COLS), F32),
            dma((10,)),
            dma((n_g, 9)),
            dma((n_g, 9)),
            dma((N_ITEMS, 16)),
            dma((N_ITEMS, 8)),
            dma((N_ITEMS, 8)),
            dma((HEADS_HERE + 1, 9)),
            dma((HEADS_HERE + 1, 9)),
            dma((8,)),
            dma((8,)),
        ],
        compiler_params=pltpu.CompilerParams(
            collective_id=0, has_side_effects=True, vmem_limit_bytes=56 << 20
        ),
        cost_estimate=pl.CostEstimate(flops=12_000_000_000, bytes_accessed=40_000_000, transcendentals=3_200_000),
    )(tokens, tangent, w_query, w_key, w_value, wo)
    return tuple(
        pl.pallas_call(
            hand_on,
            out_shape=[jax.ShapeDtypeStruct((ROWS, COLS), BF16)] * 2,
            in_specs=[vmem] * 2,
            out_specs=[vmem] * 2,
        )(layer_out, layer_tangent)
    )


def solution(mesh):
    placed = (
        P(("dp", "ctx"), "tp"),
        P(("dp", "ctx"), "tp"),
        P(None, "tp"),
        P(None, "tp"),
        P(None, "tp"),
        P("tp", None),
    )
    return jax.shard_map(
        body,
        mesh=mesh,
        in_specs=placed,
        out_specs=(P(("dp", "ctx"), "tp"), P(("dp", "ctx"), "tp")),
        check_vma=False,
    )
```

time: 124 us -> 110 us (0.89); the launches traced: 124 us -> 109 us
  Pallas kernels: 120 us -> 108 us
  local copies, waits for them, and re-layouts: 3.25 us -> 0 us
    pallas_call x1, Pallas kernels: 120 us -> 106 us  [body(): pl.pallas_call(kernel, out_shape=[jax.ShapeDtypeStruct((ROWS, COLS), BF16...]
    unnamed x2 -> x0, local copies, waits for them, and re-layouts: 3.25 us -> none
    pallas_call x0 -> x1, Pallas kernels: none -> 1.78 us  [body(): pl.pallas_call(hand_on, out_shape=[jax.ShapeDtypeStruct((ROWS, COLS), BF1...]
where the time goes in v2:
time: 110 us; the launch traced here: 109 us
  Pallas kernels  108 us (98%)
    pallas_call x1, Pallas kernels, body(): pl.pallas_call(kernel, out_shape=[jax.ShapeDtypeStruct((ROWS, COLS), BF16...  106 us

profile of v2, /device:TPU:4, one launch (start us, length us, event | category | flops | bytes accessed | tf_op | source)
XLA Modules:
  0.0 108.7 jit_solution(5817730596107789841)
XLA Ops:
  0.6 106.3 %shard_map.77 = (bf16[256,384]{1,0:T(8,128)(2,1)}, bf16[256,384]{1,0:T(8,128)(2,1)}) custom-call(bf16[256,384]{1,0:T(8,128)(2,1)} %tok.1, bf16[256,384]{1,0:T(8,128)(2,1)} %tan.1, bf16[3072,384]{1,0:T(8,128)(2,1)} %wq.1, bf16[3072,384]{1,0:T(8,128)(2,1)} %wk.1, bf16[3072,384]{1,0:T(8,128)(2,1)} %wv.1, bf16[3,128,3072]{2,1,0:T(8,128)(2,1)} %bitcast.1), custom_call_target="tpu_custom_call" | custom-call | flops 12000000000 | bytes 40000000 | tf_op jit(solution)/shard_map/pallas_call | solution.py:539
  106.9 1.8 %shard_map.78 = (bf16[256,384]{1,0:T(8,128)(2,1)}, bf16[256,384]{1,0:T(8,128)(2,1)}) custom-call(bf16[256,384]{1,0:T(8,128)(2,1)} %get-tuple-element.4.a_ref, bf16[256,384]{1,0:T(8,128)(2,1)} %get-tuple-element.5.b_ref), custom_call_target="tpu_custom_call" | custom-call | tf_op jit(solution)/shard_map/pallas_call | solution.py:573

commit v3 on v2

--- a/solution.py
+++ b/solution.py
@@ -19,10 +19,10 @@
 BF16 = jnp.bfloat16
 F32 = jnp.float32
 
-GATHERS = ((0, 0, 32), (0, 32, 32), (0, 64, 64), (0, 128, 64), (0, 192, 64), (1, 0, 128), (1, 128, 128))
-DIRECT = (False, False, False, False, False, False, False)
-DIRECT_OUT = (True, True, True, False)
-N_T = 5
+GATHERS = ((0, 0, 32), (0, 32, 32), (0, 64, 32), (0, 96, 32), (0, 128, 64), (0, 192, 64), (1, 0, 64), (1, 64, 64), (1, 128, 64), (1, 192, 64))
+DIRECT = (True, True, True, True, True, True, False, False, False, True)
+DIRECT_OUT = (False, False, True, True)
+N_T = 6
 N_ITEMS = N_T + HEADS_HERE
 
 
@@ -223,26 +223,32 @@
         for h in range(HEADS_HERE):
             qcat[h, :, pl.ds((1 - a) * HD, HD)] = res[:, h * HD : (h + 1) * HD]
 
+    ones = jnp.ones((2 * ROWS, HD), BF16)
+
+    def wide(stat_rows):
+        return jnp.concatenate([stat_rows] * (2 * ROWS // HD), axis=1)
+
     def attend(h, chip, first):
         c0 = chip * 2
         kk = kvt[pl.ds(c0, 2), h, 0].reshape(2 * ROWS, HD)
         vv = kvt[pl.ds(c0, 2), h, 1].reshape(2 * ROWS, HD)
+        vcat = jnp.concatenate([vv, ones], axis=1)
         for blk in range(2):
             rows = pl.ds(blk * 128, 128)
             s = dot_nt(qcat[h, rows, pl.ds(HD, HD)], kk)
-            top = jnp.max(s, axis=1, keepdims=True)
+            top = jnp.broadcast_to(jnp.max(s, axis=1, keepdims=True), (128, HD))
             if not first:
-                old = stat[h, 0, rows, :][:, :1]
+                old = stat[h, 0, rows, :]
                 top = jnp.maximum(old, top)
-            p = jnp.exp2((s - top) * (FACTOR * LOG2E))
-            l_new = jnp.sum(p, axis=1, keepdims=True)
-            v_new = dot_nn(p.astype(BF16), vv)
+                keep = jnp.exp2((old - top) * (FACTOR * LOG2E))
+            p = jnp.exp2((s - wide(top)) * (FACTOR * LOG2E)).astype(BF16)
+            res = dot_nn(p, vcat)
+            v_new, l_new = res[:, :HD], res[:, HD:]
             if not first:
-                keep = jnp.exp2((old - top) * (FACTOR * LOG2E))
-                l_new += stat[h, 1, rows, :][:, :1] * keep
+                l_new += stat[h, 1, rows, :] * keep
                 v_new += acc_v[h, rows, :] * keep
-            stat[h, 0, rows, :] = jnp.broadcast_to(top, (128, HD))
-            stat[h, 1, rows, :] = jnp.broadcast_to(l_new, (128, HD))
+            stat[h, 0, rows, :] = top
+            stat[h, 1, rows, :] = l_new
             acc_v[h, rows, :] = v_new
 
     def attend_dot(h, chip, first):
@@ -252,36 +258,31 @@
         kd = kvd[h, pl.ds(c0, 2), 0].reshape(2 * ROWS, HD)
         vd = kvd[h, pl.ds(c0, 2), 1].reshape(2 * ROWS, HD)
         kcat = jnp.concatenate([kk, kd], axis=1)
-        for blk in range(2):
-            rows = pl.ds(blk * 128, 128)
-            qq = qcat[h, rows, :]
-            s = dot_nt(qq[:, HD:], kk)
-            sd = dot_nt(qq, kcat)
-            p = jnp.exp2((s - stat[h, 0, rows, :][:, :1]) * (FACTOR * LOG2E))
-            w = p * sd
-            t_new = jnp.sum(w, axis=1, keepdims=True)
-            w_new = dot_nn(w.astype(BF16), vv) * FACTOR + dot_nn(p.astype(BF16), vd)
-            if not first:
-                t_new += stat[h, 2, rows, :][:, :1]
-                w_new += acc_w[h, rows, :]
-            stat[h, 2, rows, :] = jnp.broadcast_to(t_new, (128, HD))
-            acc_w[h, rows, :] = w_new
+        vcat = jnp.concatenate([vv, ones], axis=1)
+        qq = qcat[h]
+        s = dot_nt(qq[:, HD:], kk)
+        sd = dot_nt(qq, kcat)
+        p = jnp.exp2((s - wide(stat[h, 0])) * (FACTOR * LOG2E))
+        res = dot_nn((p * sd).astype(BF16), vcat)
+        w_new = res[:, :HD] * FACTOR + dot_nn(p.astype(BF16), vd)
+        t_new = res[:, HD:]
+        if not first:
+            t_new += stat[h, 2]
+            w_new += acc_w[h]
+        stat[h, 2] = t_new
+        acc_w[h] = w_new
 
     me_chip = ctx // 2
 
     def arrivals(d):
         return (0,) if d == 0 else ((2 * d - 1, 2 * d) if d < 4 else (7,))
 
-    def over(attending, h, d):
+    def chips(d):
         if d == 0:
-            attending(h, me_chip, True)
-        elif d == 4:
-            attending(h, lax.rem(me_chip + 4, 8), False)
-        else:
-            def both(k, carry):
-                attending(h, lax.rem(me_chip + 8 - d + 2 * d * k, 8), False)
-                return carry
-            lax.fori_loop(0, 2, both, 0)
+            return (me_chip,)
+        if d == 4:
+            return (lax.rem(me_chip + 4, 8),)
+        return (lax.rem(me_chip + 8 - d, 8), lax.rem(me_chip + d, 8))
 
     def t_got(d):
         for j in arrivals(d):
@@ -292,11 +293,14 @@
         for j in arrivals(d):
             sib_got(N_T + h, j)
 
-    def stage(h, d):
-        over(attend, h, d)
+    def stage(d):
+        for chip in chips(d):
+            for h in range(HEADS_HERE):
+                attend(h, chip, d == 0)
 
     def stage_dot(h, d):
-        over(attend_dot, h, d)
+        for chip in chips(d):
+            attend_dot(h, chip, d == 0)
 
     def close():
         for h in range(HEADS_HERE):
@@ -356,167 +360,154 @@
     G[0].start()
     G[1].start()
     G[2].start()
-    G[0].fwd(0)
-    G[0].fwd(1)
+    G[3].start()
+    G[4].start()
     kvw_wait()
-    G[1].fwd(0)
-    G[1].fwd(1)
-    G[0].fwd(2)
-    G[3].start()
-    G[0].fwd(3)
-    G[2].fwd(0)
-    G[2].fwd(1)
-    G[1].fwd(2)
-    G[1].fwd(3)
-    G[4].start()
-    G[3].fwd(1)
-    G[2].fwd(2)
-    G[3].fwd(0)
-    G[2].fwd(3)
     make_t(0)
     own(0)
+    G[5].start()
     make_t(1)
-    G[4].fwd(0)
-    G[3].fwd(2)
-    G[4].fwd(1)
     own(1)
-    local[1].wait()
-    G[5].start()
-    G[3].fwd(3)
     hop(0, 1)
     make_t(2)
     own(2)
-    G[4].fwd(2)
+    local[1].wait()
+    G[6].start()
     hop(1, 1)
-    G[4].fwd(3)
+    make_t(3)
+    own(3)
     hop(0, 2)
-    G[5].fwd(1)
-    G[5].fwd(0)
     hop(2, 1)
-    G[6].start()
-    make_t(3)
+    G[7].start()
     hop(1, 2)
-    G[5].fwd(2)
-    own(3)
+    hop(3, 1)
     make_t(4)
+    own(4)
     hop(0, 3)
+    G[8].start()
+    hop(2, 2)
+    hop(1, 3)
+    G[6].fwd(0)
+    hop(3, 2)
+    G[6].fwd(1)
+    make_t(5)
     local[8].wait()
     queries(0)
-    G[5].fwd(3)
-    own(4)
-    hop(2, 2)
-    G[6].fwd(0)
-    G[6].fwd(1)
-    hop(1, 3)
+    G[6].fwd(2)
+    own(5)
+    G[7].fwd(0)
+    G[7].fwd(1)
+    hop(4, 1)
+    G[6].fwd(3)
+    hop(0, 4)
+    G[9].start()
+    hop(2, 3)
     t_got(0)
-    stage(0, 0)
-    stage(1, 0)
+    stage(0)
+    hop(1, 4)
+    G[8].fwd(0)
+    G[7].fwd(2)
+    G[8].fwd(1)
+    hop(3, 3)
+    G[7].fwd(3)
+    hop(5, 1)
     weights_send(0)
-    stage(2, 0)
-    hop(3, 1)
-    G[6].fwd(2)
-    hop(0, 4)
+    G[8].fwd(2)
+    G[8].fwd(3)
+    t_got(1)
+    stage(1)
+    hop(4, 2)
+    hop(3, 4)
+    hop(2, 4)
     weights_send(1)
-    G[6].fwd(3)
-    hop(4, 1)
-    t_got(1)
-    stage(0, 1)
-    hop(1, 4)
-    hop(2, 3)
+    weights_send(2)
+    weights_send(3)
+    hop(5, 2)
     d_gathered()
     keys_values_d(0)
+    own(6)
     keys_values_d(1)
-    hop(3, 2)
     keys_values_d(2)
-    queries(1)
-    weights_send(2)
-    stage(1, 1)
-    hop(4, 2)
-    hop(2, 4)
-    stage(2, 1)
-    weights_send(3)
-    own(5)
     t_got(2)
-    stage(0, 2)
-    hop(3, 3)
-    stage(1, 2)
     hop(4, 3)
     d_got(0, 0)
     weights_send(4)
-    stage(2, 2)
+    stage(2)
+    own(7)
+    hop(5, 3)
+    weights_send(5)
+    queries(1)
+    hop(6, 1)
+    d_got(1, 0)
     t_got(3)
-    stage(0, 3)
-    hop(5, 1)
-    weights_send(5)
-    stage(1, 3)
-    hop(3, 4)
-    stage(2, 3)
+    stage(3)
     hop(4, 4)
-    own(6)
+    weights_send(6)
     d_got(0, 1)
-    weights_send(6)
+    hop(7, 1)
+    hop(5, 4)
+    d_got(1, 1)
     t_got(4)
-    stage(0, 4)
-    hop(5, 2)
-    d_got(1, 0)
-    stage(1, 4)
-    stage(2, 4)
+    stage(4)
     close()
     A[3].start()
+    hop(6, 2)
+    stage_dot(0, 0)
+    stage_dot(0, 1)
+    stage_dot(1, 0)
+    stage_dot(1, 1)
+    own(8)
+    hop(7, 2)
     d_got(0, 2)
-    stage_dot(0, 0)
-    hop(6, 1)
-    stage_dot(0, 1)
     stage_dot(0, 2)
-    hop(5, 3)
-    d_got(1, 1)
-    stage_dot(1, 0)
-    own(7)
-    stage_dot(1, 1)
-    A[3].fwd(0)
-    A[3].fwd(1)
-    hop(6, 2)
+    weights_share()
     d_got(2, 0)
-    d_got(0, 3)
-    stage_dot(0, 3)
-    hop(5, 4)
     stage_dot(2, 0)
     d_got(1, 2)
     stage_dot(1, 2)
-    A[3].fwd(2)
-    hop(7, 1)
+    hop(6, 3)
+    weights_got()
+    d_got(0, 3)
+    stage_dot(0, 3)
+    hop(8, 1)
+    d_got(2, 1)
+    hop(7, 3)
+    stage_dot(2, 1)
+    hop(6, 4)
+    d_got(1, 3)
+    stage_dot(1, 3)
     d_got(0, 4)
     stage_dot(0, 4)
     close_dot(0)
     A[0].start()
-    weights_share()
-    hop(6, 3)
-    d_got(2, 1)
-    stage_dot(2, 1)
-    A[3].fwd(3)
-    hop(7, 2)
-    weights_got()
-    d_got(1, 3)
-    stage_dot(1, 3)
-    hop(6, 4)
+    hop(8, 2)
+    hop(7, 4)
     d_got(2, 2)
     stage_dot(2, 2)
     d_got(1, 4)
     stage_dot(1, 4)
-    hop(7, 3)
     close_dot(1)
     A[1].start()
-    A[0].finish()
-    project_dot(0)
     A[3].finish()
+    A[0].fwd(0)
+    A[0].fwd(1)
+    hop(8, 3)
     project()
+    A[0].fwd(2)
     d_got(2, 3)
     stage_dot(2, 3)
-    hop(7, 4)
+    A[1].fwd(0)
+    A[1].fwd(1)
+    A[0].fwd(3)
+    hop(8, 4)
     d_got(2, 4)
     stage_dot(2, 4)
     close_dot(2)
     A[2].start()
+    A[1].fwd(2)
+    A[0].finish()
+    project_dot(0)
+    A[1].fwd(3)
     A[1].finish()
     project_dot(1)
     A[2].finish()

time: 110 us -> 103 us (0.936)
  Pallas kernels: 108 us -> 101 us
    pallas_call x1, Pallas kernels: 106 us -> 99.4 us  [body(): pl.pallas_call(kernel, out_shape=[jax.ShapeDtypeStruct((ROWS, COLS), BF16...]
where the time goes in v3:
time: 103 us; the launch traced here: 102 us
  Pallas kernels  101 us (98%)
    pallas_call x1, Pallas kernels, body(): pl.pallas_call(kernel, out_shape=[jax.ShapeDtypeStruct((ROWS, COLS), BF16...  99.4 us

profile of v3, /device:TPU:4, one launch (start us, length us, event | category | flops | bytes accessed | tf_op | source)
XLA Modules:
  0.0 101.9 jit_solution(16168371130150390382)
XLA Ops:
  0.6 99.4 %shard_map.77 = (bf16[256,384]{1,0:T(8,128)(2,1)}, bf16[256,384]{1,0:T(8,128)(2,1)}) custom-call(bf16[256,384]{1,0:T(8,128)(2,1)} %tok.1, bf16[256,384]{1,0:T(8,128)(2,1)} %tan.1, bf16[3072,384]{1,0:T(8,128)(2,1)} %wq.1, bf16[3072,384]{1,0:T(8,128)(2,1)} %wk.1, bf16[3072,384]{1,0:T(8,128)(2,1)} %wv.1, bf16[3,128,3072]{2,1,0:T(8,128)(2,1)} %bitcast.1), custom_call_target="tpu_custom_call" | custom-call | flops 12000000000 | bytes 40000000 | tf_op jit(solution)/shard_map/pallas_call | solution.py:530
  100.1 1.8 %shard_map.78 = (bf16[256,384]{1,0:T(8,128)(2,1)}, bf16[256,384]{1,0:T(8,128)(2,1)}) custom-call(bf16[256,384]{1,0:T(8,128)(2,1)} %get-tuple-element.4.a_ref, bf16[256,384]{1,0:T(8,128)(2,1)} %get-tuple-element.5.b_ref), custom_call_target="tpu_custom_call" | custom-call | tf_op jit(solution)/shard_map/pallas_call | solution.py:564

commit v4 on v3

--- a/solution.py
+++ b/solution.py
@@ -19,9 +19,9 @@
 BF16 = jnp.bfloat16
 F32 = jnp.float32
 
-GATHERS = ((0, 0, 32), (0, 32, 32), (0, 64, 32), (0, 96, 32), (0, 128, 64), (0, 192, 64), (1, 0, 64), (1, 64, 64), (1, 128, 64), (1, 192, 64))
+GATHERS = ((0, 0, 32), (0, 32, 32), (0, 64, 32), (0, 96, 64), (0, 160, 64), (0, 224, 32), (1, 0, 64), (1, 64, 64), (1, 128, 64), (1, 192, 64))
 DIRECT = (True, True, True, True, True, True, False, False, False, True)
-DIRECT_OUT = (False, False, True, True)
+DIRECT_OUT = (False, False, True, False)
 N_T = 6
 N_ITEMS = N_T + HEADS_HERE
 
@@ -125,8 +125,8 @@
             arrived(self.part(slot, part), self.ssem(j), self.rsem(j), xn)
 
         def start(self):
-            for j, dev in enumerate(peers if self.direct else peers[:5]):
-                self.go(tp, 0, j, dev)
+            for j in (6, 5, 3, 4, 0, 1, 2) if self.direct else (3, 4, 1, 2, 0):
+                self.go(tp, 0, j, peers[j])
 
         def fwd(self, k):
             self.got(back[1 + k], 0, 1 + k)
@@ -360,119 +360,123 @@
     G[0].start()
     G[1].start()
     G[2].start()
-    G[3].start()
-    G[4].start()
     kvw_wait()
     make_t(0)
     own(0)
-    G[5].start()
+    G[3].start()
     make_t(1)
     own(1)
     hop(0, 1)
     make_t(2)
     own(2)
+    G[4].start()
+    hop(1, 1)
+    hop(0, 2)
+    hop(2, 1)
+    make_t(3)
+    own(3)
+    G[5].start()
+    hop(1, 2)
     local[1].wait()
     G[6].start()
-    hop(1, 1)
-    make_t(3)
-    own(3)
-    hop(0, 2)
-    hop(2, 1)
+    hop(0, 3)
+    hop(2, 2)
     G[7].start()
-    hop(1, 2)
-    hop(3, 1)
     make_t(4)
     own(4)
-    hop(0, 3)
+    hop(3, 1)
+    hop(1, 3)
+    make_t(5)
+    hop(0, 4)
+    own(5)
     G[8].start()
-    hop(2, 2)
-    hop(1, 3)
-    G[6].fwd(0)
-    hop(3, 2)
-    G[6].fwd(1)
-    make_t(5)
+    hop(2, 3)
+    G[6].fwd(2)
     local[8].wait()
     queries(0)
-    G[6].fwd(2)
-    own(5)
+    G[6].fwd(0)
+    G[6].fwd(1)
+    G[6].fwd(3)
+    t_got(0)
+    stage(0)
+    hop(4, 1)
+    G[9].start()
     G[7].fwd(0)
     G[7].fwd(1)
-    hop(4, 1)
-    G[6].fwd(3)
-    hop(0, 4)
-    G[9].start()
-    hop(2, 3)
-    t_got(0)
-    stage(0)
+    G[7].fwd(2)
+    hop(3, 2)
+    G[7].fwd(3)
     hop(1, 4)
     G[8].fwd(0)
-    G[7].fwd(2)
     G[8].fwd(1)
-    hop(3, 3)
-    G[7].fwd(3)
     hop(5, 1)
+    hop(2, 4)
+    G[8].fwd(2)
     weights_send(0)
-    G[8].fwd(2)
-    G[8].fwd(3)
     t_got(1)
     stage(1)
+    G[8].fwd(3)
     hop(4, 2)
-    hop(3, 4)
-    hop(2, 4)
     weights_send(1)
     weights_send(2)
     weights_send(3)
+    hop(3, 3)
     hop(5, 2)
     d_gathered()
     keys_values_d(0)
     own(6)
     keys_values_d(1)
+    hop(4, 3)
     keys_values_d(2)
+    hop(3, 4)
+    d_got(0, 0)
     t_got(2)
-    hop(4, 3)
-    d_got(0, 0)
     weights_send(4)
     stage(2)
-    own(7)
     hop(5, 3)
     weights_send(5)
     queries(1)
-    hop(6, 1)
-    d_got(1, 0)
+    own(7)
+    weights_send(6)
     t_got(3)
     stage(3)
+    hop(6, 1)
     hop(4, 4)
-    weights_send(6)
+    d_got(1, 0)
+    hop(5, 4)
     d_got(0, 1)
-    hop(7, 1)
-    hop(5, 4)
-    d_got(1, 1)
     t_got(4)
     stage(4)
+    stage_dot(1, 0)
+    hop(7, 1)
     close()
-    A[3].start()
-    hop(6, 2)
     stage_dot(0, 0)
     stage_dot(0, 1)
-    stage_dot(1, 0)
+    A[3].start()
+    d_got(1, 1)
     stage_dot(1, 1)
+    hop(6, 2)
+    weights_share()
+    d_got(0, 2)
+    stage_dot(0, 2)
     own(8)
     hop(7, 2)
-    d_got(0, 2)
-    stage_dot(0, 2)
-    weights_share()
+    hop(6, 3)
+    A[3].fwd(2)
     d_got(2, 0)
     stage_dot(2, 0)
+    weights_got()
     d_got(1, 2)
     stage_dot(1, 2)
-    hop(6, 3)
-    weights_got()
     d_got(0, 3)
     stage_dot(0, 3)
     hop(8, 1)
+    A[3].fwd(0)
+    A[3].fwd(1)
+    A[3].fwd(3)
     d_got(2, 1)
+    stage_dot(2, 1)
     hop(7, 3)
-    stage_dot(2, 1)
     hop(6, 4)
     d_got(1, 3)
     stage_dot(1, 3)
@@ -481,33 +485,33 @@
     close_dot(0)
     A[0].start()
     hop(8, 2)
+    A[3].finish()
+    project()
     hop(7, 4)
     d_got(2, 2)
     stage_dot(2, 2)
     d_got(1, 4)
     stage_dot(1, 4)
+    A[0].fwd(2)
     close_dot(1)
     A[1].start()
-    A[3].finish()
     A[0].fwd(0)
     A[0].fwd(1)
     hop(8, 3)
-    project()
-    A[0].fwd(2)
+    A[0].fwd(3)
     d_got(2, 3)
     stage_dot(2, 3)
+    hop(8, 4)
+    A[1].fwd(2)
+    A[1].fwd(1)
     A[1].fwd(0)
-    A[1].fwd(1)
-    A[0].fwd(3)
-    hop(8, 4)
+    A[1].fwd(3)
     d_got(2, 4)
     stage_dot(2, 4)
     close_dot(2)
     A[2].start()
-    A[1].fwd(2)
     A[0].finish()
     project_dot(0)
-    A[1].fwd(3)
     A[1].finish()
     project_dot(1)
     A[2].finish()

time: 103 us -> 102 us (level)
  no operation moved by 1% of the time
where the time goes in v4:
time: 102 us; the launch traced here: 101 us
  Pallas kernels  100 us (98%)
    pallas_call x1, Pallas kernels, body(): pl.pallas_call(kernel, out_shape=[jax.ShapeDtypeStruct((ROWS, COLS), BF16...  98.6 us

profile of v4, /device:TPU:4, one launch (start us, length us, event | category | flops | bytes accessed | tf_op | source)
XLA Modules:
  0.0 101.0 jit_solution(11363008146124539248)
XLA Ops:
  0.6 98.6 %shard_map.77 = (bf16[256,384]{1,0:T(8,128)(2,1)}, bf16[256,384]{1,0:T(8,128)(2,1)}) custom-call(bf16[256,384]{1,0:T(8,128)(2,1)} %tok.1, bf16[256,384]{1,0:T(8,128)(2,1)} %tan.1, bf16[3072,384]{1,0:T(8,128)(2,1)} %wq.1, bf16[3072,384]{1,0:T(8,128)(2,1)} %wk.1, bf16[3072,384]{1,0:T(8,128)(2,1)} %wv.1, bf16[3,128,3072]{2,1,0:T(8,128)(2,1)} %bitcast.1), custom_call_target="tpu_custom_call" | custom-call | flops 12000000000 | bytes 40000000 | tf_op jit(solution)/shard_map/pallas_call | solution.py:534
  99.3 1.8 %shard_map.78 = (bf16[256,384]{1,0:T(8,128)(2,1)}, bf16[256,384]{1,0:T(8,128)(2,1)}) custom-call(bf16[256,384]{1,0:T(8,128)(2,1)} %get-tuple-element.4.a_ref, bf16[256,384]{1,0:T(8,128)(2,1)} %get-tuple-element.5.b_ref), custom_call_target="tpu_custom_call" | custom-call | tf_op jit(solution)/shard_map/pallas_call | solution.py:568

commit v5 on v3

--- a/solution.py
+++ b/solution.py
@@ -19,11 +19,12 @@
 BF16 = jnp.bfloat16
 F32 = jnp.float32
 
-GATHERS = ((0, 0, 32), (0, 32, 32), (0, 64, 32), (0, 96, 32), (0, 128, 64), (0, 192, 64), (1, 0, 64), (1, 64, 64), (1, 128, 64), (1, 192, 64))
-DIRECT = (True, True, True, True, True, True, False, False, False, True)
-DIRECT_OUT = (False, False, True, True)
+GATHERS = ((0, 0, 32), (0, 32, 32), (0, 64, 32), (0, 96, 64), (0, 160, 64), (0, 224, 32), (1, 0, 64), (1, 64, 64), (1, 128, 128))
+DIRECT = (True, True, True, False, False, False, False, True, True)
+DIRECT_OUT = (False, True, True, False)
 N_T = 6
-N_ITEMS = N_T + HEADS_HERE
+PIECES = ((0, 0, 128), (0, 128, 128), (1, 0, 256), (2, 0, 64), (2, 64, 192))
+N_ITEMS = N_T + len(PIECES)
 
 
 def dot_nt(a, b):
@@ -94,14 +95,15 @@
         pl.semaphore_signal(barrier, inc=1, device_id=dev, device_id_type=MESH)
     pl.semaphore_wait(barrier, len(greet))
 
-    sent = []
-
     def send(src, dst, ssem, rsem, dev):
-        c = pltpu.make_async_remote_copy(
+        pltpu.make_async_remote_copy(
             src_ref=src, dst_ref=dst, send_sem=ssem, recv_sem=rsem, device_id=dev, device_id_type=MESH
-        )
-        c.start()
-        sent.append(c)
+        ).start()
+
+    def left(ref, ssem, rsem):
+        pltpu.make_async_remote_copy(
+            src_ref=ref, dst_ref=ref, send_sem=ssem, recv_sem=rsem, device_id=xn, device_id_type=MESH
+        ).wait_send()
 
     def arrived(ref, ssem, rsem, dev):
         pltpu.make_async_remote_copy(
@@ -109,8 +111,9 @@
         ).wait_recv()
 
     class Gather:
-        def __init__(self, view, ssem, rsem, n, direct):
-            self.view, self.ssem, self.rsem, self.n, self.direct = view, ssem, rsem, n, direct
+        def __init__(self, view, blocks, ssem, rsem, n, direct):
+            self.view, self.blocks, self.n, self.direct = view, blocks, n, direct
+            self.ssem, self.rsem = ssem, rsem
 
         def part(self, slot, part):
             half = self.n // 2
@@ -119,41 +122,38 @@
 
         def go(self, slot, part, j, dev):
             ref = self.part(slot, part)
-            send(ref, ref, self.ssem(j), self.rsem(j), dev)
-
-        def got(self, slot, part, j):
-            arrived(self.part(slot, part), self.ssem(j), self.rsem(j), xn)
+            send(ref, ref, self.ssem(0), self.rsem(j), dev)
 
         def start(self):
-            for j, dev in enumerate(peers if self.direct else peers[:5]):
-                self.go(tp, 0, j, dev)
+            for j in (6, 5, 3, 4, 0, 1, 2) if self.direct else (3, 4, 1, 2, 0):
+                self.go(tp, 0, 0 if self.direct else j, peers[j])
 
         def fwd(self, k):
-            self.got(back[1 + k], 0, 1 + k)
-            self.go(back[1 + k], 1 + k % 2, 5 + k, (yp, ym)[k % 2])
+            arrived(self.part(back[1 + k], 0), self.ssem(0), self.rsem(1 + k), xn)
+            self.go(back[1 + k], 1 + k % 2, 0, (yp, ym)[k % 2])
 
         def finish(self):
-            if self.direct:
-                for j in range(len(peers)):
-                    self.got(back[j], 0, j)
-            else:
-                self.got(s_x, 0, 0)
-                for k, slot in enumerate((s_f, s_f, s_xf, s_xf)):
-                    self.got(slot, 1 + k % 2, 5 + k)
+            arrived(self.blocks(7 if self.direct else 3), self.ssem(0), self.rsem(0), xn)
+
+        def done(self):
+            left(self.blocks(7), self.ssem(0), self.rsem(0))
 
     def acts(g):
         a, r0, n = GATHERS[g]
         return Gather(
             lambda slot, lo, cnt: xg.at[a, pl.ds(r0 + lo, cnt), cols(slot, COLS)],
+            lambda cnt: xg.at[a, pl.ds(r0, n), pl.ds(0, cnt * COLS)],
             lambda j: g_send.at[g, j], lambda j: g_recv.at[g, j], n, DIRECT[g],
         )
 
     def heads_out(h):
         if h < HEADS_HERE:
             view = lambda slot, lo, cnt: at.at[h, pl.ds(ROWS + lo, cnt), cols(slot, HD)]
+            blocks = lambda cnt: at.at[h, pl.ds(ROWS, ROWS), pl.ds(0, cnt * HD)]
         else:
             view = lambda slot, lo, cnt: at.at[:, pl.ds(lo, cnt), cols(slot, HD)]
-        return Gather(view, lambda j: a_send.at[h, j], lambda j: a_recv.at[h, j], ROWS, DIRECT_OUT[h])
+            blocks = lambda cnt: at.at[:, pl.ds(0, ROWS), pl.ds(0, cnt * HD)]
+        return Gather(view, blocks, lambda j: a_send.at[h, j], lambda j: a_recv.at[h, j], ROWS, DIRECT_OUT[h])
 
     def piece(i, c, part):
         if i < N_T:
@@ -161,9 +161,10 @@
             if part == 0:
                 return kvt.at[c, :, :, pl.ds(r0, n)]
             return kvt.at[c, :, part - 1, pl.ds(r0, n)]
+        h, r0, n = PIECES[i - N_T]
         if part == 0:
-            return kvd.at[i - N_T, c]
-        return kvd.at[i - N_T, c, part - 1]
+            return kvd.at[h, c, :, pl.ds(r0, n)]
+        return kvd.at[h, c, part - 1, pl.ds(r0, n)]
 
     def minus(d):
         return lax.rem(ctx + CTX - 2 * d, CTX)
@@ -173,14 +174,17 @@
 
     def ring_send(i, c, part, j, dev):
         ref = piece(i, c, part)
-        send(ref, ref, z_send.at[i, j], z_recv.at[i, j], dev)
+        send(ref, ref, z_send.at[i], z_recv.at[i, j], dev)
+
+    def shared(i):
+        return 0 if i < N_T else 1 + PIECES[i - N_T][0]
 
     def sib_send(i, c, j):
         ref = piece(i, c, 0)
-        send(ref, ref, z_send.at[i, 8 + j], s_recv.at[i, j], sib)
+        send(ref, ref, z_send.at[i], s_recv.at[shared(i), j], sib)
 
     def ring_got(i, c, part, j):
-        arrived(piece(i, c, part), z_send.at[i, j], z_recv.at[i, j], zp)
+        arrived(piece(i, c, part), z_send.at[i], z_recv.at[i, j], zp)
 
     def own(i):
         ring_send(i, ctx, 0, 0, zp)
@@ -200,11 +204,21 @@
             ring_got(i, plus(4), 2, 7)
             sib_send(i, plus(4), 7)
 
-    def sib_got(i, j):
+    def sib_got(group, j):
         d = (j + 1) // 2
         pair = ctx + 1 - 2 * core
         c = lax.rem(pair + CTX - 2 * d, CTX) if j % 2 else lax.rem(pair + 2 * d, CTX)
-        arrived(piece(i, c, 0), z_send.at[i, 8 + j], s_recv.at[i, j], sib)
+        ref = kvt.at[c] if group == 0 else kvd.at[group - 1, c]
+        arrived(ref, z_send.at[0], s_recv.at[group, j], sib)
+
+    def ring_done(i):
+        if i < N_T:
+            _, r0, n = GATHERS[i]
+            ref = kvt.at[pl.ds(0, 15), :, :, pl.ds(r0, n)]
+        else:
+            h, r0, n = PIECES[i - N_T]
+            ref = kvd.at[h, pl.ds(0, 15), :, pl.ds(r0, n)]
+        left(ref, z_send.at[i], z_recv.at[i, 0])
 
     def keys_values_t(g):
         _, r0, n = GATHERS[g]
@@ -286,12 +300,11 @@
 
     def t_got(d):
         for j in arrivals(d):
-            for t in range(N_T):
-                sib_got(t, j)
+            sib_got(0, j)
 
     def d_got(h, d):
         for j in arrivals(d):
-            sib_got(N_T + h, j)
+            sib_got(1 + h, j)
 
     def stage(d):
         for chip in chips(d):
@@ -329,17 +342,16 @@
     def weights_send(j):
         send(
             wo.at[:, pl.ds(core * 64, 64), cols(slots[j], COLS)], wt.at[:, tp, core],
-            p_send.at[j], p_recv.at[j], peers[j],
+            p_send.at[0], p_recv.at[0], peers[j],
         )
 
     def weights_share():
-        for j in range(len(peers)):
-            arrived(wt.at[:, back[j], core], p_send.at[j], p_recv.at[j], peers[j])
+        arrived(wt.at[:, pl.ds(0, 7), core], p_send.at[0], p_recv.at[0], xn)
         local[9].wait()
-        send(wt.at[:, :, core], wt.at[:, :, core], p_send.at[7], p_recv.at[7], sib)
+        send(wt.at[:, :, core], wt.at[:, :, core], p_send.at[1], p_recv.at[1], sib)
 
     def weights_got():
-        arrived(wt.at[:, :, 1 - core], p_send.at[7], p_recv.at[7], sib)
+        arrived(wt.at[:, :, 1 - core], p_send.at[1], p_recv.at[1], sib)
 
     G = [acts(g) for g in range(len(GATHERS))]
     A = [heads_out(h) for h in range(HEADS_HERE + 1)]
@@ -360,160 +372,177 @@
     G[0].start()
     G[1].start()
     G[2].start()
-    G[3].start()
-    G[4].start()
     kvw_wait()
     make_t(0)
     own(0)
-    G[5].start()
+    G[3].start()
     make_t(1)
     own(1)
+    G[4].start()
+    make_t(2)
     hop(0, 1)
-    make_t(2)
     own(2)
+    G[3].fwd(2)
+    G[3].fwd(0)
+    G[3].fwd(1)
+    G[5].start()
+    hop(1, 1)
+    G[3].fwd(3)
     local[1].wait()
     G[6].start()
-    hop(1, 1)
+    G[4].fwd(0)
+    G[4].fwd(1)
+    hop(0, 2)
+    G[4].fwd(2)
+    hop(2, 1)
+    G[4].fwd(3)
+    G[5].fwd(1)
+    G[5].fwd(0)
+    hop(1, 2)
     make_t(3)
     own(3)
-    hop(0, 2)
-    hop(2, 1)
+    G[5].fwd(3)
+    G[5].fwd(2)
     G[7].start()
-    hop(1, 2)
-    hop(3, 1)
+    hop(0, 3)
+    G[6].fwd(1)
+    G[6].fwd(0)
+    hop(2, 2)
+    G[6].fwd(2)
     make_t(4)
+    hop(1, 3)
     own(4)
-    hop(0, 3)
-    G[8].start()
-    hop(2, 2)
-    hop(1, 3)
-    G[6].fwd(0)
-    hop(3, 2)
-    G[6].fwd(1)
     make_t(5)
+    own(5)
+    G[6].fwd(3)
     local[8].wait()
     queries(0)
-    G[6].fwd(2)
-    own(5)
-    G[7].fwd(0)
-    G[7].fwd(1)
-    hop(4, 1)
-    G[6].fwd(3)
     hop(0, 4)
-    G[9].start()
+    hop(3, 1)
+    G[8].start()
     hop(2, 3)
     t_got(0)
     stage(0)
     hop(1, 4)
-    G[8].fwd(0)
-    G[7].fwd(2)
-    G[8].fwd(1)
-    hop(3, 3)
-    G[7].fwd(3)
+    hop(4, 1)
     hop(5, 1)
     weights_send(0)
-    G[8].fwd(2)
-    G[8].fwd(3)
+    hop(3, 2)
     t_got(1)
     stage(1)
-    hop(4, 2)
-    hop(3, 4)
     hop(2, 4)
     weights_send(1)
     weights_send(2)
+    hop(4, 2)
     weights_send(3)
     hop(5, 2)
     d_gathered()
     keys_values_d(0)
     own(6)
     keys_values_d(1)
+    own(7)
     keys_values_d(2)
+    own(8)
+    hop(3, 3)
+    weights_send(4)
+    queries(1)
+    weights_send(5)
+    hop(4, 3)
+    hop(5, 3)
+    d_got(0, 0)
     t_got(2)
-    hop(4, 3)
-    d_got(0, 0)
-    weights_send(4)
     stage(2)
-    own(7)
-    hop(5, 3)
-    weights_send(5)
-    queries(1)
     hop(6, 1)
     d_got(1, 0)
+    weights_send(6)
     t_got(3)
     stage(3)
+    hop(7, 1)
+    hop(8, 1)
+    d_got(0, 1)
+    hop(3, 4)
     hop(4, 4)
-    weights_send(6)
-    d_got(0, 1)
-    hop(7, 1)
     hop(5, 4)
     d_got(1, 1)
+    own(9)
+    hop(6, 2)
     t_got(4)
     stage(4)
+    hop(7, 2)
     close()
     A[3].start()
-    hop(6, 2)
-    stage_dot(0, 0)
-    stage_dot(0, 1)
     stage_dot(1, 0)
     stage_dot(1, 1)
-    own(8)
-    hop(7, 2)
+    own(10)
+    weights_share()
     d_got(0, 2)
+    stage_dot(0, 0)
+    hop(8, 2)
+    stage_dot(0, 1)
+    hop(9, 1)
     stage_dot(0, 2)
-    weights_share()
+    hop(6, 3)
     d_got(2, 0)
     stage_dot(2, 0)
+    hop(7, 3)
+    weights_got()
     d_got(1, 2)
     stage_dot(1, 2)
-    hop(6, 3)
-    weights_got()
+    hop(10, 1)
     d_got(0, 3)
+    A[3].fwd(2)
     stage_dot(0, 3)
-    hop(8, 1)
     d_got(2, 1)
-    hop(7, 3)
+    hop(8, 3)
     stage_dot(2, 1)
+    A[3].fwd(0)
+    hop(9, 2)
+    A[3].fwd(3)
     hop(6, 4)
+    A[3].fwd(1)
+    hop(7, 4)
     d_got(1, 3)
     stage_dot(1, 3)
+    hop(10, 2)
     d_got(0, 4)
     stage_dot(0, 4)
     close_dot(0)
     A[0].start()
-    hop(8, 2)
-    hop(7, 4)
+    hop(8, 4)
+    hop(9, 3)
     d_got(2, 2)
     stage_dot(2, 2)
     d_got(1, 4)
     stage_dot(1, 4)
     close_dot(1)
     A[1].start()
+    hop(10, 3)
+    hop(9, 4)
     A[3].finish()
+    project()
+    A[0].fwd(2)
     A[0].fwd(0)
     A[0].fwd(1)
-    hop(8, 3)
-    project()
-    A[0].fwd(2)
+    A[0].fwd(3)
     d_got(2, 3)
     stage_dot(2, 3)
-    A[1].fwd(0)
-    A[1].fwd(1)
-    A[0].fwd(3)
-    hop(8, 4)
+    hop(10, 4)
     d_got(2, 4)
     stage_dot(2, 4)
     close_dot(2)
     A[2].start()
-    A[1].fwd(2)
+    A[1].finish()
     A[0].finish()
     project_dot(0)
-    A[1].fwd(3)
-    A[1].finish()
     project_dot(1)
     A[2].finish()
     project_dot(2)
-    for c in sent:
-        c.wait_send()
+    for gather in G + A:
+        gather.done()
+    for i in range(N_ITEMS):
+        ring_done(i)
+    left(wt.at[:, pl.ds(0, 7), core], p_send.at[0], p_recv.at[0])
+    left(wt.at[:, :, core], p_send.at[1], p_recv.at[1])
 
 
 def hand_on(a_ref, b_ref, c_ref, d_ref):
@@ -547,13 +576,13 @@
             dma((10,)),
             dma((n_g, 9)),
             dma((n_g, 9)),
-            dma((N_ITEMS, 16)),
+            dma((N_ITEMS,)),
             dma((N_ITEMS, 8)),
-            dma((N_ITEMS, 8)),
+            dma((1 + HEADS_HERE, 8)),
             dma((HEADS_HERE + 1, 9)),
             dma((HEADS_HERE + 1, 9)),
-            dma((8,)),
-            dma((8,)),
+            dma((2,)),
+            dma((2,)),
         ],
         compiler_params=pltpu.CompilerParams(
             collective_id=0, has_side_effects=True, vmem_limit_bytes=56 << 20

time: 103 us -> 99.3 us (0.964)
  Pallas kernels: 101 us -> 97.2 us
    pallas_call x1, Pallas kernels: 99.4 us -> 95.4 us  [body(): pl.pallas_call(kernel, out_shape=[jax.ShapeDtypeStruct((ROWS, COLS), BF16...]
where the time goes in v5:
time: 99.3 us; the launch traced here: 97.9 us
  Pallas kernels  97.2 us (98%)
    pallas_call x1, Pallas kernels, body(): pl.pallas_call(kernel, out_shape=[jax.ShapeDtypeStruct((ROWS, COLS), BF16...  95.4 us

profile of v5, /device:TPU:4, one launch (start us, length us, event | category | flops | bytes accessed | tf_op | source)
XLA Modules:
  0.0 97.9 jit_solution(2444348882382451749)
XLA Ops:
  0.6 95.4 %shard_map.77 = (bf16[256,384]{1,0:T(8,128)(2,1)}, bf16[256,384]{1,0:T(8,128)(2,1)}) custom-call(bf16[256,384]{1,0:T(8,128)(2,1)} %tok.1, bf16[256,384]{1,0:T(8,128)(2,1)} %tan.1, bf16[3072,384]{1,0:T(8,128)(2,1)} %wq.1, bf16[3072,384]{1,0:T(8,128)(2,1)} %wk.1, bf16[3072,384]{1,0:T(8,128)(2,1)} %wv.1, bf16[3,128,3072]{2,1,0:T(8,128)(2,1)} %bitcast.1), custom_call_target="tpu_custom_call" | custom-call | flops 12000000000 | bytes 40000000 | tf_op jit(solution)/shard_map/pallas_call | solution.py:559
  96.1 1.8 %shard_map.78 = (bf16[256,384]{1,0:T(8,128)(2,1)}, bf16[256,384]{1,0:T(8,128)(2,1)}) custom-call(bf16[256,384]{1,0:T(8,128)(2,1)} %get-tuple-element.4.a_ref, bf16[256,384]{1,0:T(8,128)(2,1)} %get-tuple-element.5.b_ref), custom_call_target="tpu_custom_call" | custom-call | tf_op jit(solution)/shard_map/pallas_call | solution.py:593

commit v6 on v5

--- a/solution.py
+++ b/solution.py
@@ -19,11 +19,11 @@
 BF16 = jnp.bfloat16
 F32 = jnp.float32
 
-GATHERS = ((0, 0, 32), (0, 32, 32), (0, 64, 32), (0, 96, 64), (0, 160, 64), (0, 224, 32), (1, 0, 64), (1, 64, 64), (1, 128, 128))
-DIRECT = (True, True, True, False, False, False, False, True, True)
+GATHERS = ((0, 0, 32), (0, 32, 32), (0, 64, 32), (0, 96, 64), (0, 160, 64), (0, 224, 32), (1, 0, 256))
+DIRECT = (True, True, True, True, True, True, False)
 DIRECT_OUT = (False, True, True, False)
 N_T = 6
-PIECES = ((0, 0, 128), (0, 128, 128), (1, 0, 256), (2, 0, 64), (2, 64, 192))
+PIECES = ((0, 0, 128), (0, 128, 128), (1, 0, 192), (1, 192, 64), (2, 0, 192), (2, 192, 64))
 N_ITEMS = N_T + len(PIECES)
 
 
@@ -368,181 +368,176 @@
         for g in range(N_T, len(GATHERS)):
             G[g].finish()
 
+    def sent_earlier():
+        for gather in G + [A[0], A[1], A[3]]:
+            gather.done()
+        for i in range(N_ITEMS):
+            ring_done(i)
+        left(wt.at[:, pl.ds(0, 7), core], p_send.at[0], p_recv.at[0])
+        left(wt.at[:, :, core], p_send.at[1], p_recv.at[1])
+
     local[0].wait()
     G[0].start()
     G[1].start()
     G[2].start()
+    G[3].start()
     kvw_wait()
     make_t(0)
     own(0)
-    G[3].start()
+    G[4].start()
     make_t(1)
     own(1)
-    G[4].start()
+    hop(0, 1)
     make_t(2)
-    hop(0, 1)
     own(2)
-    G[3].fwd(2)
-    G[3].fwd(0)
-    G[3].fwd(1)
     G[5].start()
     hop(1, 1)
-    G[3].fwd(3)
+    hop(0, 2)
     local[1].wait()
     G[6].start()
-    G[4].fwd(0)
-    G[4].fwd(1)
-    hop(0, 2)
-    G[4].fwd(2)
     hop(2, 1)
-    G[4].fwd(3)
-    G[5].fwd(1)
-    G[5].fwd(0)
+    make_t(3)
     hop(1, 2)
-    make_t(3)
     own(3)
-    G[5].fwd(3)
-    G[5].fwd(2)
-    G[7].start()
     hop(0, 3)
+    hop(2, 2)
+    hop(1, 3)
+    make_t(4)
+    own(4)
+    hop(3, 1)
+    make_t(5)
+    own(5)
+    local[8].wait()
+    queries(0)
+    hop(2, 3)
+    hop(1, 4)
+    t_got(0)
+    hop(0, 4)
+    stage(0)
+    hop(4, 1)
+    G[6].fwd(2)
+    hop(3, 2)
+    weights_send(0)
+    hop(5, 1)
+    hop(2, 4)
     G[6].fwd(1)
     G[6].fwd(0)
-    hop(2, 2)
-    G[6].fwd(2)
-    make_t(4)
-    hop(1, 3)
-    own(4)
-    make_t(5)
-    own(5)
+    t_got(1)
     G[6].fwd(3)
-    local[8].wait()
-    queries(0)
-    hop(0, 4)
-    hop(3, 1)
-    G[8].start()
-    hop(2, 3)
-    t_got(0)
-    stage(0)
-    hop(1, 4)
-    hop(4, 1)
-    hop(5, 1)
-    weights_send(0)
-    hop(3, 2)
-    t_got(1)
     stage(1)
-    hop(2, 4)
+    hop(4, 2)
     weights_send(1)
     weights_send(2)
-    hop(4, 2)
+    hop(3, 3)
     weights_send(3)
     hop(5, 2)
+    weights_send(4)
     d_gathered()
     keys_values_d(0)
     own(6)
+    own(7)
     keys_values_d(1)
-    own(7)
+    hop(3, 4)
+    queries(1)
+    hop(5, 3)
+    t_got(2)
+    hop(4, 3)
     keys_values_d(2)
+    hop(6, 1)
+    stage(2)
+    hop(7, 1)
+    hop(5, 4)
     own(8)
-    hop(3, 3)
-    weights_send(4)
-    queries(1)
+    d_got(0, 0)
+    hop(4, 4)
     weights_send(5)
-    hop(4, 3)
-    hop(5, 3)
-    d_got(0, 0)
-    t_got(2)
-    stage(2)
-    hop(6, 1)
-    d_got(1, 0)
     weights_send(6)
     t_got(3)
     stage(3)
-    hop(7, 1)
-    hop(8, 1)
     d_got(0, 1)
-    hop(3, 4)
-    hop(4, 4)
-    hop(5, 4)
-    d_got(1, 1)
     own(9)
     hop(6, 2)
+    hop(7, 2)
     t_got(4)
     stage(4)
-    hop(7, 2)
     close()
     A[3].start()
+    d_got(0, 2)
+    hop(8, 1)
+    d_got(1, 0)
     stage_dot(1, 0)
+    hop(9, 1)
+    stage_dot(0, 0)
+    stage_dot(0, 1)
+    hop(6, 3)
+    stage_dot(0, 2)
+    hop(7, 3)
+    d_got(1, 1)
     stage_dot(1, 1)
     own(10)
     weights_share()
-    d_got(0, 2)
-    stage_dot(0, 0)
     hop(8, 2)
-    stage_dot(0, 1)
-    hop(9, 1)
-    stage_dot(0, 2)
-    hop(6, 3)
+    d_got(0, 3)
+    stage_dot(0, 3)
+    hop(9, 2)
+    hop(6, 4)
+    hop(7, 4)
+    A[3].fwd(2)
+    weights_got()
+    own(11)
+    d_got(1, 2)
+    hop(10, 1)
+    d_got(0, 4)
+    A[3].fwd(3)
+    stage_dot(0, 4)
     d_got(2, 0)
+    close_dot(0)
+    A[0].start()
     stage_dot(2, 0)
-    hop(7, 3)
-    weights_got()
-    d_got(1, 2)
+    hop(8, 3)
+    A[3].fwd(0)
+    hop(9, 3)
+    A[3].fwd(1)
+    hop(11, 1)
     stage_dot(1, 2)
-    hop(10, 1)
-    d_got(0, 3)
-    A[3].fwd(2)
-    stage_dot(0, 3)
-    d_got(2, 1)
-    hop(8, 3)
-    stage_dot(2, 1)
-    A[3].fwd(0)
-    hop(9, 2)
-    A[3].fwd(3)
-    hop(6, 4)
-    A[3].fwd(1)
-    hop(7, 4)
     d_got(1, 3)
     stage_dot(1, 3)
     hop(10, 2)
-    d_got(0, 4)
-    stage_dot(0, 4)
-    close_dot(0)
-    A[0].start()
+    d_got(2, 1)
+    stage_dot(2, 1)
     hop(8, 4)
-    hop(9, 3)
-    d_got(2, 2)
-    stage_dot(2, 2)
+    A[0].fwd(0)
+    A[0].fwd(1)
+    hop(9, 4)
+    hop(11, 2)
+    A[0].fwd(3)
+    A[0].fwd(2)
     d_got(1, 4)
     stage_dot(1, 4)
     close_dot(1)
+    hop(10, 3)
     A[1].start()
-    hop(10, 3)
-    hop(9, 4)
+    hop(11, 3)
+    d_got(2, 2)
+    stage_dot(2, 2)
     A[3].finish()
     project()
-    A[0].fwd(2)
-    A[0].fwd(0)
-    A[0].fwd(1)
-    A[0].fwd(3)
     d_got(2, 3)
+    hop(10, 4)
+    hop(11, 4)
     stage_dot(2, 3)
-    hop(10, 4)
+    A[0].finish()
+    project_dot(0)
     d_got(2, 4)
     stage_dot(2, 4)
     close_dot(2)
     A[2].start()
     A[1].finish()
-    A[0].finish()
-    project_dot(0)
     project_dot(1)
+    sent_earlier()
     A[2].finish()
     project_dot(2)
-    for gather in G + A:
-        gather.done()
-    for i in range(N_ITEMS):
-        ring_done(i)
-    left(wt.at[:, pl.ds(0, 7), core], p_send.at[0], p_recv.at[0])
-    left(wt.at[:, :, core], p_send.at[1], p_recv.at[1])
+    A[2].done()
 
 
 def hand_on(a_ref, b_ref, c_ref, d_ref):

time: 99.3 us -> 99.3 us (level)
  no operation moved by 1% of the time
where the time goes in v6:
time: 99.3 us; the launch traced here: 97.9 us
  Pallas kernels  97.3 us (98%)
    pallas_call x1, Pallas kernels, body(): pl.pallas_call(kernel, out_shape=[jax.ShapeDtypeStruct((ROWS, COLS), BF16...  95.5 us

profile of v6, /device:TPU:4, one launch (start us, length us, event | category | flops | bytes accessed | tf_op | source)
XLA Modules:
  0.0 97.9 jit_solution(8234777939837992020)
XLA Ops:
  0.6 95.5 %shard_map.77 = (bf16[256,384]{1,0:T(8,128)(2,1)}, bf16[256,384]{1,0:T(8,128)(2,1)}) custom-call(bf16[256,384]{1,0:T(8,128)(2,1)} %tok.1, bf16[256,384]{1,0:T(8,128)(2,1)} %tan.1, bf16[3072,384]{1,0:T(8,128)(2,1)} %wq.1, bf16[3072,384]{1,0:T(8,128)(2,1)} %wk.1, bf16[3072,384]{1,0:T(8,128)(2,1)} %wv.1, bf16[3,128,3072]{2,1,0:T(8,128)(2,1)} %bitcast.1), custom_call_target="tpu_custom_call" | custom-call | flops 12000000000 | bytes 40000000 | tf_op jit(solution)/shard_map/pallas_call | solution.py:554
  96.2 1.8 %shard_map.78 = (bf16[256,384]{1,0:T(8,128)(2,1)}, bf16[256,384]{1,0:T(8,128)(2,1)}) custom-call(bf16[256,384]{1,0:T(8,128)(2,1)} %get-tuple-element.4.a_ref, bf16[256,384]{1,0:T(8,128)(2,1)} %get-tuple-element.5.b_ref), custom_call_target="tpu_custom_call" | custom-call | tf_op jit(solution)/shard_map/pallas_call | solution.py:588
